TPU v7x, 32 devices: a whole 2x2x4 slice. The times are simulated.
32 devices in a mesh: rep: 8 (over z, x), fsdp: 4 (over y, core).
Axes of the slice: x: 2, y: 2, z: 4, core: 2. Of those that a mesh axis runs over, the one named last changes fastest.
Arguments:
- tokens: bfloat16 [6144, 4096], P(('rep', 'fsdp')), may hold values from -6 to 6
- quant_weight: bfloat16 [4096, 512], P('fsdp'), may hold values from -6 to 6
- block_scales: bfloat16 [1024], P('fsdp'), may hold values from 0.0069885254 to 0.031982422
- key_grad: bfloat16 [6144, 512], P(('rep', 'fsdp')), may hold values from -6 to 6
Outputs:
- rotated: bfloat16 [6144, 512], P(('rep', 'fsdp'))
- token_grad: bfloat16 [6144, 4096], P(('rep', 'fsdp'))
- weight_grad: bfloat16 [4096, 512], P(('rep', 'fsdp'))
All inputs are finite; a program needn't handle non-finite values.
Results may differ from a plain program's by a relative error of at most 0.023.
Values may be sent and summed in bfloat16 or wider, within the bound.
A program may use at most 64 MiB of HBM per device.

v0:
```python
import math

import jax
import jax.numpy as jnp
from jax import lax
from jax.sharding import PartitionSpec as P

HEAD_DIM = 128


rope_base = 10000.0


def dequantize(quant_weight, block_scales):
    rows_per_block = quant_weight.shape[0] // block_scales.shape[0]
    scaled = quant_weight.astype(jnp.float32).reshape(
        block_scales.shape[0], rows_per_block, quant_weight.shape[1]
    )
    scaled = scaled * block_scales.astype(jnp.float32)[:, None, None]
    return scaled.reshape(quant_weight.shape).astype(jnp.bfloat16)


def rotary(projected, positions, direction):
    half_size = HEAD_DIM // 2
    steps = jnp.arange(half_size, dtype=jnp.int32).astype(jnp.float32)
    frequency = jnp.exp(steps * (-2.0 * math.log(rope_base) / HEAD_DIM))
    angles = positions[:, None] * frequency[None, :]
    cosine = jnp.cos(angles)[:, None, :]
    sine_part = direction * jnp.sin(angles)[:, None, :]
    halves = projected.reshape(projected.shape[0], -1, 2, half_size)
    leading = halves[:, :, 0]
    trailing = halves[:, :, 1]
    turned = jnp.stack(
        [leading * cosine - trailing * sine_part, trailing * cosine + leading * sine_part], axis=2
    )
    return turned.reshape(projected.shape)


def partial_rows(source, proj_grad):
    return lax.dot_general(
        source, proj_grad, (((0,), (0,)), ((), ())), preferred_element_type=jnp.float32
    )


def body(tokens, quant_weight, block_scales, key_grad):
    row_count = tokens.shape[0]
    all_codes, all_scales = (
        lax.all_gather(quant_weight, "fsdp", axis=0, tiled=True),
        lax.all_gather(block_scales, "fsdp", axis=0, tiled=True),
    )
    weight = dequantize(all_codes, all_scales)
    positions = (
        lax.axis_index("fsdp") * row_count + jnp.arange(row_count, dtype=jnp.int32)
    ).astype(jnp.float32)
    projected = jnp.dot(tokens, weight, preferred_element_type=jnp.float32)
    rotated = rotary(projected, positions, 1.0).astype(jnp.bfloat16)
    proj_grad = rotary(key_grad.astype(jnp.float32), positions, -1.0).astype(jnp.bfloat16)
    token_grad = lax.dot_general(
        proj_grad, weight, (((1,), (1,)), ((), ())), preferred_element_type=jnp.float32
    ).astype(jnp.bfloat16)
    total_rows = weight.shape[0]
    fsdp_size = lax.axis_size("fsdp")
    rep_size = lax.axis_size("rep")
    share = total_rows // (fsdp_size * rep_size)
    reordered = (
        tokens.reshape(row_count, rep_size, fsdp_size, share)
        .transpose(0, 2, 1, 3)
        .reshape(row_count, total_rows)
    )
    group_sum = lax.psum_scatter(
        partial_rows(reordered, proj_grad).astype(jnp.bfloat16),
        "fsdp",
        scatter_dimension=0,
        tiled=True,
    ).astype(jnp.float32)
    summed = lax.psum_scatter(group_sum, "rep", scatter_dimension=0, tiled=True)
    weight_grad = (summed * (1.0 / math.sqrt(row_count * fsdp_size * rep_size))).astype(
        jnp.bfloat16
    )
    return (rotated, token_grad, weight_grad)


def solution(mesh):
    return jax.shard_map(
        body,
        mesh=mesh,
        in_specs=(P(("rep", "fsdp"), None), P("fsdp", None), P("fsdp"), P(("rep", "fsdp"), None)),
        out_specs=(P(("rep", "fsdp"), None), P(("rep", "fsdp"), None), P(("rep", "fsdp"), None)),
        check_vma=False,
    )
```

profile of v0, /device:TPU:0, one launch (start us, length us, event | category | flops | bytes accessed | tf_op | source)
XLA Modules:
  0.0 179.2 jit_solution(11102427041047569482)
XLA Ops:
  7.2 0.0 reduce-scatter.3.cloned.1.call-start
  7.2 1.1 copy.14
  8.4 2.8 %reshape.121 = bf16[192,8,4,128]{3,2,1,0:T(4,128)(2,1)S(1)} reshape(bf16[192,4096]{1,0:T(8,128)(2,1)} %param.4) | data formatting | bytes 3145728 | tf_op jit(solution)/shard_map/reshape | solution.py:66
  11.2 0.3 copy.15
  11.5 0.3 broadcast_multiply_fusion
  11.8 0.1 multiply_subtract_fusion
  11.9 3.3 %fusion = bf16[4096,512]{0,1:T(8,128)(2,1)} fusion(bf16[192,512]{0,1:T(8,128)(2,1)S(1)} %bitcast.21, bf16[24,8,32,128]{3,2,1,0:T(8,128)(2,1)S(1)} %bitcast.19), kind=kOutput, calls=%fused_computation.2 | convolution fusion | flops 807403520 | bytes 5963776 | tf_op jit(solution)/shard_map/dot_general | solution.py:40
  15.2 0.0 reduce-scatter.3.cloned.1.call-update
  15.2 0.0 copy-start.1
  15.2 0.0 copy-start
  15.2 0.0 all-gather.3.cloned.1.call-start
  15.3 0.7 all-gather.3.cloned.1.call-update
  16.0 0.0 reduce-scatter.5.cloned.1.call-start
  16.0 46.6 %reduce-scatter.3.cloned.1.call-done = bf16[1024,512]{0,1:T(8,128)(2,1)} async-done(((bf16[4096,512]{0,1:T(8,128)(2,1)}), bf16[1024,512]{0,1:T(8,128)(2,1)}) %reduce-scatter.3.cloned.1.call-update) | async-done | bytes 1048592 | tf_op jit(solution)/shard_map/reduce_scatter | solution.py:70
  62.6 2.8 %convert_element_type.68 = f32[1024,512]{0,1:T(8,128)} convert(bf16[1024,512]{0,1:T(8,128)(2,1)} %reduce-scatter.3.cloned.1.call-done) | non-fusion elementwise | flops 524288 | bytes 3145728 | tf_op jit(solution)/shard_map/convert_element_type | solution.py:75
  65.4 0.0 reduce-scatter.5.cloned.1.call-update
  65.4 0.0 copy-done.1
  65.4 5.1 %all-gather = bf16[4,1,256]{2,1,0:T(2,128)(2,1)S(1)} all-gather(bf16[1,1,256]{2,1,0:T(2,128)(2,1)S(1)} %reshape.125), channel_id=1, replica_groups=mesh['rep'=8,'fsdp'=4] {'fsdp'}, dimensions={0}, use_global_device_ids=true | all-gather | bytes 2560 | tf_op jit(solution)/shard_map/all_gather | solution.py:49
  70.5 0.2 mul.133
  70.7 0.3 mul.134
  71.0 27.8 %all-gather.3.cloned.1.call-done = bf16[4096,512]{1,0:T(8,128)(2,1)} async-done(((bf16[1024,512]{1,0:T(8,128)(2,1)}), bf16[4096,512]{1,0:T(8,128)(2,1)}) %all-gather.3.cloned.1.call-update) | async-done | bytes 4194320 | tf_op jit(solution)/shard_map/all_gather | solution.py:48
  98.7 0.0 copy-done
  98.7 3.3 %fusion.4 = f32[192,512]{1,0:T(8,128)S(1)} fusion(bf16[192,4096]{1,0:T(8,128)(2,1)S(1)} %copy-done, bf16[4096,512]{1,0:T(8,128)(2,1)} %all-gather.3.cloned.1.call-done, f32[4096]{0:T(1024)S(1)} %mul.134), kind=kOutput, calls=%fused_computation.7 | convolution fusion | flops 811597824 | bytes 6176768 | tf_op jit(solution)/shard_map/dot_general | solution.py:55
  102.1 0.2 copy.13
  102.3 0.1 subtract_convert_fusion
  102.4 0.8 copy.16
  103.2 5.5 %convolution_convert_fusion.1 = bf16[192,4096]{1,0:T(8,128)(2,1)} fusion(bf16[192,512]{0,1:T(8,128)(2,1)S(1)} %bitcast.22, bf16[4096,512]{1,0:T(8,128)(2,1)} %all-gather.3.cloned.1.call-done, f32[4096]{0:T(1024)S(1)} %mul.134), kind=kOutput, calls=%fused_computation.3 | convolution fusion | flops 812384256 | bytes 5980160 | tf_op jit(solution)/shard_map/dot_general | solution.py:58
  108.7 62.2 %reduce-scatter.5.cloned.1.call-done = f32[128,512]{0,1:T(8,128)} async-done(((f32[1024,512]{0,1:T(8,128)}), f32[128,512]{0,1:T(8,128)}) %reduce-scatter.5.cloned.1.call-update) | async-done | bytes 262160 | tf_op jit(solution)/shard_map/reduce_scatter | solution.py:76
  170.9 1.0 multiply_convert_fusion.5
  171.9 0.8 copy.17
  (7 shorter events, 0.2 us)
Async XLA Ops:
  7.2 55.4 %reduce-scatter.3.cloned.1.call-start = ((), (), s32[]{:S(2)}) async-start(), calls=%async_computation.3 | async-start | bytes 5242880 | tf_op jit(solution)/shard_map/reduce_scatter | solution.py:70
  15.2 50.2 %copy-start.1 = (bf16[256]{0:T(256)(128)(2,1)S(1)}, bf16[256]{0:T(256)(128)(2,1)}, u32[]{:S(2)}) copy-start(bf16[256]{0:T(256)(128)(2,1)} %param.6) | copy-start | bytes 1540
  15.2 83.5 %copy-start = (bf16[192,4096]{1,0:T(8,128)(2,1)S(1)}, bf16[192,4096]{1,0:T(8,128)(2,1)}, u32[]{:S(2)}) copy-start(bf16[192,4096]{1,0:T(8,128)(2,1)} %param.4) | copy-start | bytes 4718596
  15.2 83.5 %all-gather.3.cloned.1.call-start = ((), (), s32[]{:S(2)}) async-start(), calls=%async_computation.2 | async-start | bytes 5242880 | tf_op jit(solution)/shard_map/all_gather | solution.py:48
  16.0 154.9 %reduce-scatter.5.cloned.1.call-start = ((), (), s32[]{:S(2)}) async-start(), calls=%async_computation.4 | async-start | bytes 2359296 | tf_op jit(solution)/shard_map/reduce_scatter | solution.py:76
Sparse Core Ops, SparseCore 0:
  15.3 47.2 reduce-scatter.2
  64.2 34.4 all-gather.2
  102.7 68.1 reduce-scatter.4
where the time goes:
time: 180 us; the launch traced here: 179 us
  waiting for transfers between devices  137 us (76%)
  between operations  13.9 us (8%)
  matrix products  12.1 us (7%)
  local copies, waits for them, and re-layouts  6.41 us (4%)
  blocking collectives  5.07 us (3%)
  other arithmetic  4.37 us (2%)
    reduce_scatter x1, waiting for transfers between devices, body(): summed = lax.psum_scatter(group_sum, 'rep', scatter_dimension=0, tiled=True)  62.2 us
    reduce_scatter x1, waiting for transfers between devices, body(): lax.psum_scatter(partial_rows(reordered, proj_grad).astype(jnp.bfloat16),...  46.6 us
    all_gather x1, waiting for transfers between devices, body(): lax.all_gather(quant_weight, 'fsdp', axis=0, tiled=True)  27.8 us
    dot_general x1, matrix products, body(): lax.dot_general(proj_grad, weight, (((1,), (1,)), ((), ())), preferred_el...  5.48 us
    all_gather x1, blocking collectives, body(): lax.all_gather(block_scales, 'fsdp', axis=0, tiled=True)  5.07 us
  transfers between devices with their start and end apart: 3, of which 3 were waited for; matrix products, arithmetic and copies ran while one was open for 7% of the time, Pallas kernels for 0%

commit v1 on v0

--- a/solution.py
+++ b/solution.py
@@ -3,6 +3,8 @@
 import jax
 import jax.numpy as jnp
 from jax import lax
+from jax.experimental import pallas as pl
+from jax.experimental.pallas import tpu as pltpu
 from jax.sharding import PartitionSpec as P
 
 HEAD_DIM = 128
@@ -80,9 +82,312 @@
     return (rotated, token_grad, weight_grad)
 
 
+MESH = pl.DeviceIdType.MESH
+
+
+def fused_kernel(
+    tok_ref, quant_ref, scale_ref, kg_ref,
+    rot_ref, tg_ref, wg_ref,
+    wbuf, tok_twin, pg, proj, cos_t, sin_t,
+    s_a, s_b, s_c, a1, b1, c1, a2, b2, c2, a3, b3, c3, a4, b4, c4,
+    tok_sem, pg_sem, w_send, w_recv, rs_send, rs_recv,
+):
+    rep, fsdp = lax.axis_index("rep"), lax.axis_index("fsdp")
+    x, z0, z1 = rep % 2, (rep // 2) % 2, rep // 4
+    y, c = fsdp // 2, fsdp % 2
+    twin = (rep, fsdp + 1 - 2 * c)
+    over_y = (rep, fsdp + 2 - 4 * y)
+    over_x = (rep + 1 - 2 * x, fsdp)
+    over_z0 = (rep + 2 - 4 * z0, fsdp)
+    over_z1 = (rep + 4 - 8 * z1, fsdp)
+    row_count, width = kg_ref.shape
+    shard_rows = quant_ref.shape[0]
+    piece = shard_rows // 4
+    block = wg_ref.shape[0]
+
+    barrier = pltpu.get_barrier_semaphore()
+    for other in (twin, over_y, over_x, over_z0, over_z1):
+        pl.semaphore_signal(barrier, inc=1, device_id=other, device_id_type=MESH)
+    pl.semaphore_wait(barrier, 5)
+
+    started = []
+
+    def send(src, dst, send_sem, recv_sem, to):
+        copy = pltpu.make_async_remote_copy(
+            src_ref=src, dst_ref=dst, send_sem=send_sem, recv_sem=recv_sem,
+            device_id=to, device_id_type=MESH,
+        )
+        copy.start()
+        started.append(copy)
+        return copy
+
+    def send_tokens(j, carry):
+        col = pl.multiple_of((2 * j + 1 - c) * block, block)
+        pltpu.make_async_remote_copy(
+            src_ref=tok_ref.at[:, pl.ds(col, block)], dst_ref=tok_twin.at[j],
+            send_sem=tok_sem.at[0], recv_sem=tok_sem.at[1],
+            device_id=twin, device_id_type=MESH,
+        ).start()
+        return carry
+
+    lax.fori_loop(0, 16, send_tokens, 0)
+    all_tokens = pltpu.make_async_remote_copy(
+        src_ref=tok_twin, dst_ref=tok_twin, send_sem=tok_sem.at[0], recv_sem=tok_sem.at[1],
+        device_id=twin, device_id_type=MESH,
+    )
+
+    def dequant(i):
+        rows = pl.ds(pl.multiple_of(i * piece, piece), piece)
+        n_blocks = scale_ref.shape[1]
+        per_block = shard_rows // n_blocks
+        owner = (i * piece + lax.broadcasted_iota(jnp.int32, (piece, n_blocks), 0)) // per_block
+        lane = lax.broadcasted_iota(jnp.int32, (piece, n_blocks), 1)
+        picked = jnp.where(owner == lane, scale_ref[...].astype(jnp.float32), 0.0)
+        column = jnp.sum(picked, axis=1, keepdims=True)
+        wbuf[fsdp, i] = (quant_ref[rows, :].astype(jnp.float32) * column).astype(jnp.bfloat16)
+
+    def send_w(shard, i, slot, to):
+        return send(
+            wbuf.at[shard, i], wbuf.at[shard, i], w_send.at[slot], w_recv.at[slot], to
+        )
+
+    from_y = []
+    for q in range(2):
+        dequant(2 * x + q)
+        from_y.append(send_w(fsdp, 2 * x + q, q, over_y))
+
+    shape = (row_count, HEAD_DIM)
+    half = HEAD_DIM // 2
+    lane = lax.broadcasted_iota(jnp.int32, shape, 1)
+    steps = (lane % half).astype(jnp.float32)
+    frequency = jnp.exp(steps * (-2.0 * math.log(rope_base) / HEAD_DIM))
+    place = (fsdp * row_count + lax.broadcasted_iota(jnp.int32, shape, 0)).astype(jnp.float32)
+    angles = place * frequency
+    cos_t[...] = jnp.cos(angles)
+    sine = jnp.sin(angles)
+    sin_t[...] = jnp.where(lane < half, -sine, sine)
+
+    def turn(value, direction):
+        return value * cos_t[...] + pltpu.roll(value, half, 1) * (direction * sin_t[...])
+
+    heads = width // HEAD_DIM
+    for h in range(heads):
+        cols = slice(h * HEAD_DIM, (h + 1) * HEAD_DIM)
+        pg[0, :, cols] = turn(kg_ref[:, cols].astype(jnp.float32), -1.0).astype(jnp.bfloat16)
+    pg_copy = send(pg.at[0], pg.at[1], pg_sem.at[0], pg_sem.at[1], twin)
+
+    for q in range(2):
+        dequant(2 * (1 - x) + q)
+    own_half = [
+        send(
+            wbuf.at[fsdp, pl.ds(2 * h, 2)], wbuf.at[fsdp, pl.ds(2 * h, 2)],
+            w_send.at[2 + h], w_recv.at[2 + h], twin,
+        )
+        for h in range(2)
+    ]
+
+    all_tokens.wait_recv()
+    pg_copy.wait_recv()
+
+    def blocks(bx, by, bz0):
+        def one(bz1, carry):
+            index = bz1 * 8 + bz0 * 4 + bx * 2 + by
+            col = pl.multiple_of((2 * index + c) * block, block)
+            left = jnp.concatenate([tok_ref[:, pl.ds(col, block)], tok_twin[index]], axis=0)
+            right = pg[...].reshape(2 * row_count, width)
+            total = lax.dot_general(
+                left, right, (((0,), (0,)), ((), ())), preferred_element_type=jnp.float32
+            ).astype(jnp.bfloat16)
+            quarter = block // 4
+            s_a[bx, by, bz0, bz1] = total[:quarter]
+            s_b[by, bz0, bx, bz1] = total[quarter : 2 * quarter]
+            s_c[bz0, bx, by, bz1] = total[2 * quarter :]
+            return carry
+
+        lax.fori_loop(0, 2, one, 0)
+
+    class Flow:
+        def __init__(self, index, bits, others, bufs):
+            self.index, self.bits, self.others, self.bufs = index, bits, others, bufs
+            self.copies = {}
+
+        def launch(self, stage, part):
+            bits, bufs = self.bits, self.bufs
+            slot = self.index * 8 + stage * 2 + part
+            sems = (rs_send.at[slot], rs_recv.at[slot], self.others[stage])
+            lead = 1 - bits[stage]
+            if stage == 3:
+                src, dst = bufs[3].at[lead], bufs[4]
+            else:
+                sub = 1 - bits[stage + 1] if part == 0 else bits[stage + 1]
+                src, dst = bufs[stage].at[lead, sub], bufs[stage + 1].at[sub]
+            self.copies[stage, part] = send(src, dst, *sems)
+
+        def take(self, stage, part):
+            bits, bufs = self.bits, self.bufs
+            self.copies[stage, part].wait_recv()
+            sub = 1 - bits[stage + 1] if part == 0 else bits[stage + 1]
+            mine = bufs[stage][bits[stage], sub].astype(jnp.float32)
+            bufs[stage + 1][sub] = (
+                bufs[stage + 1][sub].astype(jnp.float32) + mine
+            ).astype(jnp.bfloat16)
+            if part == 0:
+                self.launch(stage + 1, 0)
+                if stage + 1 < 3:
+                    self.launch(stage + 1, 1)
+
+        def finish(self, rows):
+            bits, bufs = self.bits, self.bufs
+            self.copies[3, 0].wait_recv()
+            total = bufs[4][...].astype(jnp.float32) + bufs[3][bits[3]].astype(jnp.float32)
+            count = row_count * lax.axis_size("rep") * lax.axis_size("fsdp")
+            wg_ref[rows, :] = (total * (1.0 / math.sqrt(count))).astype(jnp.bfloat16)
+
+    fa = Flow(0, (x, y, z0, z1), (over_x, over_y, over_z0, over_z1), (s_a, a1, a2, a3, a4))
+    fb = Flow(1, (y, z0, x, z1), (over_y, over_z0, over_x, over_z1), (s_b, b1, b2, b3, b4))
+    fc = Flow(2, (z0, x, y, z1), (over_z0, over_x, over_y, over_z1), (s_c, c1, c2, c3, c4))
+
+    blocks(1 - x, 1 - y, 1 - z0)
+    blocks(1 - x, y, 1 - z0)
+    fc.launch(0, 0)
+    blocks(1 - x, 1 - y, z0)
+    fa.launch(0, 0)
+    blocks(x, 1 - y, 1 - z0)
+    fb.launch(0, 0)
+    blocks(x, y, 1 - z0)
+    fc.launch(0, 1)
+    blocks(1 - x, y, z0)
+    fa.launch(0, 1)
+    blocks(x, 1 - y, z0)
+    fb.launch(0, 1)
+    blocks(x, y, z0)
+
+    proj[...] = jnp.zeros_like(proj)
+
+    def use(shard, first, count):
+        def one(i, carry):
+            at = first + i
+            col = pl.multiple_of(shard * shard_rows + at * piece, piece)
+            w = wbuf[shard, at]
+            tg_ref[:, pl.ds(col, piece)] = lax.dot_general(
+                pg[0], w, (((1,), (1,)), ((), ())), preferred_element_type=jnp.float32
+            ).astype(jnp.bfloat16)
+            proj[...] += jnp.dot(
+                tok_ref[:, pl.ds(col, piece)], w, preferred_element_type=jnp.float32
+            )
+            return carry
+
+        lax.fori_loop(0, count, one, 0)
+
+    side = fsdp + 2 - 4 * y
+    twin_shard = fsdp + 1 - 2 * c
+    twin_side = side + 1 - 2 * c
+
+    from_x, from_twin = [], []
+
+    def forward(q):
+        from_y[q].wait_recv()
+        from_x.append(send_w(side, 2 * x + q, 4 + q, over_x))
+        from_twin.append(send_w(side, 2 * x + q, 6 + q, twin))
+
+    def forward_x(q):
+        from_x[q].wait_recv()
+        from_twin.append(send_w(side, 2 * (1 - x) + q, 8 + q, twin))
+
+    use(fsdp, 0, 4)
+    forward(0)
+    for copy in own_half:
+        copy.wait_recv()
+    use(twin_shard, 0, 4)
+    fa.take(0, 0)
+    fa.take(0, 1)
+    forward(1)
+    fc.take(0, 0)
+    fb.take(0, 0)
+    forward_x(0)
+    fc.take(0, 1)
+    fa.take(1, 0)
+    fb.take(0, 1)
+    use(side, 2 * x, 2)
+    fa.take(1, 1)
+    fb.take(1, 0)
+    fc.take(1, 0)
+    fa.take(2, 0)
+    fb.take(1, 1)
+    fc.take(1, 1)
+    fa.take(2, 1)
+    fb.take(2, 0)
+    fc.take(2, 0)
+    fb.take(2, 1)
+    fc.take(2, 1)
+    forward_x(1)
+    from_twin[0].wait_recv()
+    from_twin[1].wait_recv()
+    use(twin_side, 2 * x, 2)
+    use(side, 2 * (1 - x), 2)
+    quarter = block // 4
+    fa.finish(slice(0, quarter))
+    fb.finish(slice(quarter, 2 * quarter))
+    fc.finish(slice(2 * quarter, block))
+    from_twin[2].wait_recv()
+    from_twin[3].wait_recv()
+    use(twin_side, 2 * (1 - x), 2)
+    for h in range(heads):
+        cols = slice(h * HEAD_DIM, (h + 1) * HEAD_DIM)
+        rot_ref[:, cols] = turn(proj[:, cols], 1.0).astype(jnp.bfloat16)
+
+    all_tokens.wait_send()
+    for copy in started:
+        copy.wait_send()
+
+
+def fused_body(tokens, quant_weight, block_scales, key_grad):
+    row_count, model = tokens.shape
+    shard_rows, width = quant_weight.shape
+    block = model // (lax.axis_size("rep") * lax.axis_size("fsdp"))
+    quarter = block // 4
+    bf16, f32 = jnp.bfloat16, jnp.float32
+    vmem = pl.BlockSpec(memory_space=pltpu.VMEM)
+    tall = (quarter, quarter, 2 * quarter)
+    flows = [
+        pltpu.VMEM((2,) * (4 - level) + (rows, width), bf16)
+        for level in range(5)
+        for rows in tall
+    ]
+    return pl.pallas_call(
+        fused_kernel,
+        out_shape=[
+            jax.ShapeDtypeStruct((row_count, width), bf16),
+            jax.ShapeDtypeStruct((row_count, model), bf16),
+            jax.ShapeDtypeStruct((block, width), bf16),
+        ],
+        in_specs=[vmem] * 4,
+        out_specs=[vmem] * 3,
+        scratch_shapes=[
+            pltpu.VMEM((4, 4, shard_rows // 4, width), bf16),
+            pltpu.VMEM((16, row_count, block), bf16),
+            pltpu.VMEM((2, row_count, width), bf16),
+            pltpu.VMEM((row_count, width), f32),
+            pltpu.VMEM((row_count, HEAD_DIM), f32),
+            pltpu.VMEM((row_count, HEAD_DIM), f32),
+            *flows,
+            pltpu.SemaphoreType.DMA((2,)),
+            pltpu.SemaphoreType.DMA((2,)),
+            pltpu.SemaphoreType.DMA((10,)),
+            pltpu.SemaphoreType.DMA((10,)),
+            pltpu.SemaphoreType.DMA((24,)),
+            pltpu.SemaphoreType.DMA((24,)),
+        ],
+        compiler_params=pltpu.CompilerParams(
+            collective_id=0, has_side_effects=True, vmem_limit_bytes=40 * 1024 * 1024
+        ),
+    )(tokens, quant_weight, block_scales.reshape(1, -1), key_grad)
+
+
 def solution(mesh):
+    paired = mesh.shape["rep"] == 8 and mesh.shape["fsdp"] == 4
     return jax.shard_map(
-        body,
+        fused_body if paired else body,
         mesh=mesh,
         in_specs=(P(("rep", "fsdp"), None), P("fsdp", None), P("fsdp"), P(("rep", "fsdp"), None)),
         out_specs=(P(("rep", "fsdp"), None), P(("rep", "fsdp"), None), P(("rep", "fsdp"), None)),

time: 180 us -> 49.5 us (0.28)
  waiting for transfers between devices: 137 us -> 0 us
  Pallas kernels: 0 us -> 42 us
  between operations: 13.9 us -> 0.64 us
  matrix products: 12.1 us -> 0 us
  blocking collectives: 5.07 us -> 0 us
  other arithmetic: 4.37 us -> 0 us
    reduce_scatter x2 -> x0, waiting for transfers between devices: 109 us -> none  [the longest x1 62.2 us: body(): summed = lax.psum_scatter(group_sum, 'rep', scatter_dimension=0, tiled=True)]
    pallas_call x0 -> x1, Pallas kernels: none -> 42 us  [fused_body(): pl.pallas_call(fused_kernel, out_shape=[jax.ShapeDtypeStruct((row_count,...]
    all_gather x1 -> x0, waiting for transfers between devices: 27.8 us -> none  [body(): lax.all_gather(quant_weight, 'fsdp', axis=0, tiled=True)]
    dot_general x3 -> x0, matrix products: 12.1 us -> none  [the longest x1 5.48 us: body(): lax.dot_general(proj_grad, weight, (((1,), (1,)), ((), ())), preferred_el...]
    all_gather x1 -> x0, blocking collectives: 5.07 us -> none  [body(): lax.all_gather(block_scales, 'fsdp', axis=0, tiled=True)]
    convert_element_type x5 -> x0, other arithmetic: 3.82 us -> none  [the longest x1 2.79 us: body(): group_sum = lax.psum_scatter(partial_rows(reordered, proj_grad).astype(jn...]
    unnamed x8 -> x9, local copies, waits for them, and re-layouts: 2.65 us -> 6.03 us
    reshape x2 -> x1, local copies, waits for them, and re-layouts: 3.1 us -> 0.66 us  [fused_body(): block_scales.reshape(1, -1)]
  transfers between devices with their start and end apart: 3 -> 0, of which waited for: 3 -> 0; matrix products, arithmetic and copies ran while one was open for 7% -> 0% of each run, Pallas kernels for 0% -> 0%
where the time goes in v1:
time: 49.5 us; the launch traced here: 49.3 us
  Pallas kernels  42 us (85%)
  local copies, waits for them, and re-layouts  6.69 us (14%)
  between operations  0.64 us (1%)
    pallas_call x1, Pallas kernels, fused_body(): pl.pallas_call(fused_kernel, out_shape=[jax.ShapeDtypeStruct((row_count,...  42 us
    unnamed x9, local copies, waits for them, and re-layouts  6.03 us

profile of v1, /device:TPU:0, one launch (start us, length us, event | category | flops | bytes accessed | tf_op | source)
XLA Modules:
  0.0 49.3 jit_solution(5600547355017280135)
XLA Ops:
  0.6 0.7 %reshape.9.scale_ref = bf16[1,256]{1,0:T(2,128)(2,1)S(1)} reshape(bf16[256]{0:T(256)(128)(2,1)} %param.6) | data formatting | bytes 1024 | tf_op jit(solution)/shard_map/reshape | solution.py:384
  1.3 0.0 copy-start
  1.3 1.4 %copy-done = bf16[192,4096]{1,0:T(8,128)(2,1)S(1)} copy-done((bf16[192,4096]{1,0:T(8,128)(2,1)S(1)}, bf16[192,4096]{1,0:T(8,128)(2,1)}, u32[]{:S(2)}) %copy-start) | copy-done | bytes 1572888
  2.7 0.0 copy-start.1
  2.7 1.2 %copy-done.1 = bf16[1024,512]{1,0:T(8,128)(2,1)S(1)} copy-done((bf16[1024,512]{1,0:T(8,128)(2,1)S(1)}, bf16[1024,512]{1,0:T(8,128)(2,1)}, u32[]{:S(2)}) %copy-start.1) | copy-done | bytes 1048600
  3.9 0.0 copy-start.2
  3.9 0.9 %copy-done.2 = bf16[192,512]{1,0:T(8,128)(2,1)S(1)} copy-done((bf16[192,512]{1,0:T(8,128)(2,1)S(1)}, bf16[192,512]{1,0:T(8,128)(2,1)}, u32[]{:S(2)}) %copy-start.2) | copy-done | bytes 196632
  4.9 42.0 %shard_map.67 = (bf16[192,512]{1,0:T(8,128)(2,1)S(1)}, bf16[192,4096]{1,0:T(8,128)(2,1)S(1)}, bf16[128,512]{1,0:T(8,128)(2,1)S(1)}) custom-call(bf16[192,4096]{1,0:T(8,128)(2,1)S(1)} %copy-done, bf16[1024,512]{1,0:T(8,128)(2,1)S(1)} %copy-done.1, bf16[1,256]{1,0:T(2,128)(2,1)S(1)} %reshape.9.scale_ref, bf16[192,512]{1,0:T(8,128)(2,1)S(1)} %copy-done.2), custom_call_target="tpu_custom_call" | custom-call | tf_op jit(solution)/shard_map/pallas_call | solution.py:357
  46.8 0.7 %copy.10 = bf16[192,512]{1,0:T(8,128)(2,1)} copy(bf16[192,512]{1,0:T(8,128)(2,1)S(1)} %get-tuple-element.6) | data formatting | bytes 393216
  47.5 1.1 %copy.11 = bf16[192,4096]{1,0:T(8,128)(2,1)} copy(bf16[192,4096]{1,0:T(8,128)(2,1)S(1)} %get-tuple-element.7) | data formatting | bytes 3145728
  48.7 0.7 %copy.12 = bf16[128,512]{1,0:T(8,128)(2,1)} copy(bf16[128,512]{1,0:T(8,128)(2,1)S(1)} %get-tuple-element.8) | data formatting | bytes 262144
Async XLA Ops:
  1.3 1.4 %copy-start = (bf16[192,4096]{1,0:T(8,128)(2,1)S(1)}, bf16[192,4096]{1,0:T(8,128)(2,1)}, u32[]{:S(2)}) copy-start(bf16[192,4096]{1,0:T(8,128)(2,1)} %tok_ref.1) | copy-start | bytes 4718596
  2.7 1.2 %copy-start.1 = (bf16[1024,512]{1,0:T(8,128)(2,1)S(1)}, bf16[1024,512]{1,0:T(8,128)(2,1)}, u32[]{:S(2)}) copy-start(bf16[1024,512]{1,0:T(8,128)(2,1)} %quant_ref.1) | copy-start | bytes 3145732
  3.9 0.9 %copy-start.2 = (bf16[192,512]{1,0:T(8,128)(2,1)S(1)}, bf16[192,512]{1,0:T(8,128)(2,1)}, u32[]{:S(2)}) copy-start(bf16[192,512]{1,0:T(8,128)(2,1)} %kg_ref.1) | copy-start | bytes 589828

commit v2 on v1

v2 whole, which is shorter than its diff:
```python
import math

import jax
import jax.numpy as jnp
from jax import lax
from jax.experimental import pallas as pl
from jax.experimental.pallas import tpu as pltpu
from jax.sharding import PartitionSpec as P

HEAD_DIM = 128


rope_base = 10000.0


def dequantize(quant_weight, block_scales):
    rows_per_block = quant_weight.shape[0] // block_scales.shape[0]
    scaled = quant_weight.astype(jnp.float32).reshape(
        block_scales.shape[0], rows_per_block, quant_weight.shape[1]
    )
    scaled = scaled * block_scales.astype(jnp.float32)[:, None, None]
    return scaled.reshape(quant_weight.shape).astype(jnp.bfloat16)


def rotary(projected, positions, direction):
    half_size = HEAD_DIM // 2
    steps = jnp.arange(half_size, dtype=jnp.int32).astype(jnp.float32)
    frequency = jnp.exp(steps * (-2.0 * math.log(rope_base) / HEAD_DIM))
    angles = positions[:, None] * frequency[None, :]
    cosine = jnp.cos(angles)[:, None, :]
    sine_part = direction * jnp.sin(angles)[:, None, :]
    halves = projected.reshape(projected.shape[0], -1, 2, half_size)
    leading = halves[:, :, 0]
    trailing = halves[:, :, 1]
    turned = jnp.stack(
        [leading * cosine - trailing * sine_part, trailing * cosine + leading * sine_part], axis=2
    )
    return turned.reshape(projected.shape)


def partial_rows(source, proj_grad):
    return lax.dot_general(
        source, proj_grad, (((0,), (0,)), ((), ())), preferred_element_type=jnp.float32
    )


def body(tokens, quant_weight, block_scales, key_grad):
    row_count = tokens.shape[0]
    all_codes, all_scales = (
        lax.all_gather(quant_weight, "fsdp", axis=0, tiled=True),
        lax.all_gather(block_scales, "fsdp", axis=0, tiled=True),
    )
    weight = dequantize(all_codes, all_scales)
    positions = (
        lax.axis_index("fsdp") * row_count + jnp.arange(row_count, dtype=jnp.int32)
    ).astype(jnp.float32)
    projected = jnp.dot(tokens, weight, preferred_element_type=jnp.float32)
    rotated = rotary(projected, positions, 1.0).astype(jnp.bfloat16)
    proj_grad = rotary(key_grad.astype(jnp.float32), positions, -1.0).astype(jnp.bfloat16)
    token_grad = lax.dot_general(
        proj_grad, weight, (((1,), (1,)), ((), ())), preferred_element_type=jnp.float32
    ).astype(jnp.bfloat16)
    total_rows = weight.shape[0]
    fsdp_size = lax.axis_size("fsdp")
    rep_size = lax.axis_size("rep")
    share = total_rows // (fsdp_size * rep_size)
    reordered = (
        tokens.reshape(row_count, rep_size, fsdp_size, share)
        .transpose(0, 2, 1, 3)
        .reshape(row_count, total_rows)
    )
    group_sum = lax.psum_scatter(
        partial_rows(reordered, proj_grad).astype(jnp.bfloat16),
        "fsdp",
        scatter_dimension=0,
        tiled=True,
    ).astype(jnp.float32)
    summed = lax.psum_scatter(group_sum, "rep", scatter_dimension=0, tiled=True)
    weight_grad = (summed * (1.0 / math.sqrt(row_count * fsdp_size * rep_size))).astype(
        jnp.bfloat16
    )
    return (rotated, token_grad, weight_grad)


MESH = pl.DeviceIdType.MESH


def fused_kernel(
    tok_hbm, quant_hbm, scale_ref, kg_hbm,
    rot_ref, tg_hbm, wg_ref,
    tok_ref, quant_ref, kg_ref, tg_ref,
    wbuf, tok_twin, pg, proj, cos_t, sin_t,
    s_a, s_b, a1, b1, a2, b2, a3, b3, a4, b4,
    load_sem, store_sem, tok_sem, pg_sem, w_send, w_recv, rs_send, rs_recv,
):
    rep, fsdp = lax.axis_index("rep"), lax.axis_index("fsdp")
    x, z0, z1 = rep % 2, (rep // 2) % 2, rep // 4
    y, c = fsdp // 2, fsdp % 2
    twin = (rep, fsdp + 1 - 2 * c)
    over_y = (rep, fsdp + 2 - 4 * y)
    over_x = (rep + 1 - 2 * x, fsdp)
    over_z0 = (rep + 2 - 4 * z0, fsdp)
    over_z1 = (rep + 4 - 8 * z1, fsdp)
    row_count, width = kg_ref.shape
    shard_rows = quant_ref.shape[0]
    piece = shard_rows // 4
    part = shard_rows // 8
    block = wg_ref.shape[0]
    here = 2 * x + z0

    load_quant = pltpu.make_async_copy(quant_hbm, quant_ref, load_sem.at[0])
    load_quant.start()
    load_kg = pltpu.make_async_copy(kg_hbm, kg_ref, load_sem.at[1])
    load_kg.start()
    load_tok = pltpu.make_async_copy(tok_hbm, tok_ref, load_sem.at[2])
    load_tok.start()

    barrier = pltpu.get_barrier_semaphore()
    for other in (twin, over_y, over_x, over_z0, over_z1):
        pl.semaphore_signal(barrier, inc=1, device_id=other, device_id_type=MESH)

    def dequant(i):
        rows = pl.ds(pl.multiple_of(i * part, part), part)
        n_blocks = scale_ref.shape[1]
        per_block = shard_rows // n_blocks
        owner = (i * part + lax.broadcasted_iota(jnp.int32, (part, n_blocks), 0)) // per_block
        lane = lax.broadcasted_iota(jnp.int32, (part, n_blocks), 1)
        picked = jnp.where(owner == lane, scale_ref[...].astype(jnp.float32), 0.0)
        column = jnp.sum(picked, axis=1, keepdims=True)
        wbuf[fsdp, i] = (quant_ref[rows, :].astype(jnp.float32) * column).astype(jnp.bfloat16)

    load_quant.wait()
    dequant(2 * here)
    dequant(2 * here + 1)
    pl.semaphore_wait(barrier, 5)

    started = []

    def send(src, dst, send_sem, recv_sem, to):
        copy = pltpu.make_async_remote_copy(
            src_ref=src, dst_ref=dst, send_sem=send_sem, recv_sem=recv_sem,
            device_id=to, device_id_type=MESH,
        )
        copy.start()
        started.append(copy)
        return copy

    def send_w(shard, i, slot, to):
        return send(
            wbuf.at[shard, i], wbuf.at[shard, i], w_send.at[slot], w_recv.at[slot], to
        )

    from_y = [send_w(fsdp, 2 * here + q, q, over_y) for q in range(2)]

    def send_tokens(j, carry):
        col = pl.multiple_of((2 * j + 1 - c) * block, block)
        pltpu.make_async_remote_copy(
            src_ref=tok_hbm.at[:, pl.ds(col, block)], dst_ref=tok_twin.at[j],
            send_sem=tok_sem.at[0], recv_sem=tok_sem.at[1],
            device_id=twin, device_id_type=MESH,
        ).start()
        return carry

    lax.fori_loop(0, 16, send_tokens, 0)
    all_tokens = pltpu.make_async_remote_copy(
        src_ref=tok_twin, dst_ref=tok_twin, send_sem=tok_sem.at[0], recv_sem=tok_sem.at[1],
        device_id=twin, device_id_type=MESH,
    )

    shape = (row_count, HEAD_DIM)
    half = HEAD_DIM // 2
    lane = lax.broadcasted_iota(jnp.int32, shape, 1)
    steps = (lane % half).astype(jnp.float32)
    frequency = jnp.exp(steps * (-2.0 * math.log(rope_base) / HEAD_DIM))
    place = (fsdp * row_count + lax.broadcasted_iota(jnp.int32, shape, 0)).astype(jnp.float32)
    angles = place * frequency
    cos_t[...] = jnp.cos(angles)
    sine = jnp.sin(angles)
    sin_t[...] = jnp.where(lane < half, -sine, sine)

    def turn(value, direction):
        return value * cos_t[...] + pltpu.roll(value, half, 1) * (direction * sin_t[...])

    heads = width // HEAD_DIM
    load_kg.wait()
    for h in range(heads):
        cols = slice(h * HEAD_DIM, (h + 1) * HEAD_DIM)
        pg[0, :, cols] = turn(kg_ref[:, cols].astype(jnp.float32), -1.0).astype(jnp.bfloat16)
    pg_copy = send(pg.at[0], pg.at[1], pg_sem.at[0], pg_sem.at[1], twin)

    def dequant_other(i, carry):
        other = (2 * here + 2 + i) % 8
        dequant(other)
        return carry

    lax.fori_loop(0, 6, dequant_other, 0)
    load_tok.wait()
    all_tokens.wait_recv()
    pg_copy.wait_recv()
    own = send(wbuf.at[fsdp], wbuf.at[fsdp], w_send.at[16], w_recv.at[16], twin)

    def blocks(bx, by):
        def one(bz, carry):
            bz0, bz1 = bz // 2, bz % 2
            index = bz1 * 8 + bz0 * 4 + bx * 2 + by
            col = pl.multiple_of((2 * index + c) * block, block)
            left = jnp.concatenate([tok_ref[:, pl.ds(col, block)], tok_twin[index]], axis=0)
            right = pg[...].reshape(2 * row_count, width)
            total = lax.dot_general(
                left, right, (((0,), (0,)), ((), ())), preferred_element_type=jnp.float32
            ).astype(jnp.bfloat16)
            s_a[bx, by, bz0, bz1] = total[: block // 2]
            s_b[by, bx, bz0, bz1] = total[block // 2 :]
            return carry

        lax.fori_loop(0, 4, one, 0)

    class Flow:
        def __init__(self, index, bits, others, bufs):
            self.index, self.bits, self.others, self.bufs = index, bits, others, bufs
            self.copies = {}

        def launch(self, stage, turn_of):
            bits, bufs = self.bits, self.bufs
            slot = self.index * 8 + stage * 2 + turn_of
            sems = (rs_send.at[slot], rs_recv.at[slot], self.others[stage])
            lead = 1 - bits[stage]
            if stage == 3:
                src, dst = bufs[3].at[lead], bufs[4]
            else:
                sub = 1 - bits[stage + 1] if turn_of == 0 else bits[stage + 1]
                src, dst = bufs[stage].at[lead, sub], bufs[stage + 1].at[sub]
            self.copies[stage, turn_of] = send(src, dst, *sems)

        def take(self, stage, turn_of):
            bits, bufs = self.bits, self.bufs
            self.copies[stage, turn_of].wait_recv()
            sub = 1 - bits[stage + 1] if turn_of == 0 else bits[stage + 1]
            mine = bufs[stage][bits[stage], sub].astype(jnp.float32)
            bufs[stage + 1][sub] = (
                bufs[stage + 1][sub].astype(jnp.float32) + mine
            ).astype(jnp.bfloat16)
            if turn_of == 0:
                self.launch(stage + 1, 0)
                if stage + 1 < 3:
                    self.launch(stage + 1, 1)

        def finish(self, rows):
            bits, bufs = self.bits, self.bufs
            self.copies[3, 0].wait_recv()
            total = bufs[4][...].astype(jnp.float32) + bufs[3][bits[3]].astype(jnp.float32)
            count = row_count * lax.axis_size("rep") * lax.axis_size("fsdp")
            wg_ref[rows, :] = (total * (1.0 / math.sqrt(count))).astype(jnp.bfloat16)

    fa = Flow(0, (x, y, z0, z1), (over_x, over_y, over_z0, over_z1), (s_a, a1, a2, a3, a4))
    fb = Flow(1, (y, x, z0, z1), (over_y, over_x, over_z0, over_z1), (s_b, b1, b2, b3, b4))

    def use(shard, at):
        col = pl.multiple_of(shard * shard_rows + at * piece, piece)
        cols = pl.ds(col, piece)
        w = wbuf[shard, pl.ds(2 * at, 2)].reshape(piece, width)
        tg_ref[:, cols] = lax.dot_general(
            pg[0], w, (((1,), (1,)), ((), ())), preferred_element_type=jnp.float32
        ).astype(jnp.bfloat16)
        pltpu.make_async_copy(tg_ref.at[:, cols], tg_hbm.at[:, cols], store_sem.at[0]).start()
        proj[...] += jnp.dot(tok_ref[:, cols], w, preferred_element_type=jnp.float32)

    def use_all(shard):
        def one(i, carry):
            use(shard, i)
            return carry

        lax.fori_loop(0, 4, one, 0)

    side = fsdp + 2 - 4 * y
    twin_shard = fsdp + 1 - 2 * c
    twin_side = side + 1 - 2 * c
    there_x, there_z, there = 2 * (1 - x) + z0, 2 * x + 1 - z0, 3 - here
    from_x, from_z, from_twin = [], [], []

    def pass_y(q):
        i = 2 * here + q
        from_y[q].wait_recv()
        from_x.append(send_w(side, i, 2 + q, over_x))
        from_z.append(send_w(side, i, 4 + q, over_z0))
        from_twin.append(send_w(side, i, 8 + q, twin))

    def pass_x(q):
        i = 2 * there_x + q
        from_x[q].wait_recv()
        from_z.append(send_w(side, i, 6 + q, over_z0))
        from_twin.append(send_w(side, i, 10 + q, twin))

    def pass_z(q):
        i = 2 * (there_z if q < 2 else there) + q % 2
        from_z[q].wait_recv()
        from_twin.append(send_w(side, i, 12 + q, twin))

    proj[...] = jnp.zeros_like(proj)
    blocks(1 - x, 1 - y)
    fa.launch(0, 0)
    fb.launch(0, 0)
    pass_y(0)
    blocks(1 - x, y)
    blocks(x, 1 - y)
    pass_y(1)
    fa.launch(0, 1)
    fb.launch(0, 1)
    blocks(x, y)
    use_all(fsdp)
    pass_x(0)
    own.wait_recv()
    use(twin_shard, 0)
    use(twin_shard, 1)
    pass_z(0)
    use(twin_shard, 2)
    use(twin_shard, 3)
    pass_x(1)
    pass_z(1)
    fa.take(0, 0)
    fb.take(0, 0)
    use(side, here)
    pass_z(2)
    use(side, there_x)
    use(side, there_z)
    fb.take(0, 1)
    fa.take(0, 1)
    pass_z(3)
    fa.take(1, 0)
    fb.take(1, 0)
    use(side, there)
    for copy in from_twin[:2]:
        copy.wait_recv()
    use(twin_side, here)
    fa.take(1, 1)
    fb.take(1, 1)
    fa.take(2, 0)
    fb.take(2, 0)
    for copy in from_twin[2:]:
        copy.wait_recv()
    use(twin_side, there_x)
    use(twin_side, there_z)
    fa.take(2, 1)
    fb.take(2, 1)
    use(twin_side, there)
    for h in range(heads):
        cols = slice(h * HEAD_DIM, (h + 1) * HEAD_DIM)
        rot_ref[:, cols] = turn(proj[:, cols], 1.0).astype(jnp.bfloat16)
    fa.finish(slice(0, block // 2))
    fb.finish(slice(block // 2, block))

    pltpu.make_async_copy(tg_ref, tg_hbm, store_sem.at[0]).wait()
    all_tokens.wait_send()
    for copy in started:
        copy.wait_send()


def fused_body(tokens, quant_weight, block_scales, key_grad):
    row_count, model = tokens.shape
    shard_rows, width = quant_weight.shape
    block = model // (lax.axis_size("rep") * lax.axis_size("fsdp"))
    bf16, f32 = jnp.bfloat16, jnp.float32
    vmem = pl.BlockSpec(memory_space=pltpu.VMEM)
    hbm = pl.BlockSpec(memory_space=pltpu.HBM)
    flows = [
        pltpu.VMEM((2,) * (4 - level) + (block // 2, width), bf16)
        for level in range(5)
        for _ in range(2)
    ]
    return pl.pallas_call(
        fused_kernel,
        out_shape=[
            jax.ShapeDtypeStruct((row_count, width), bf16),
            jax.ShapeDtypeStruct((row_count, model), bf16),
            jax.ShapeDtypeStruct((block, width), bf16),
        ],
        in_specs=[hbm, hbm, vmem, hbm],
        out_specs=[vmem, hbm, vmem],
        scratch_shapes=[
            pltpu.VMEM((row_count, model), bf16),
            pltpu.VMEM((shard_rows, width), bf16),
            pltpu.VMEM((row_count, width), bf16),
            pltpu.VMEM((row_count, model), bf16),
            pltpu.VMEM((4, 8, shard_rows // 8, width), bf16),
            pltpu.VMEM((16, row_count, block), bf16),
            pltpu.VMEM((2, row_count, width), bf16),
            pltpu.VMEM((row_count, width), f32),
            pltpu.VMEM((row_count, HEAD_DIM), f32),
            pltpu.VMEM((row_count, HEAD_DIM), f32),
            *flows,
            pltpu.SemaphoreType.DMA((3,)),
            pltpu.SemaphoreType.DMA((1,)),
            pltpu.SemaphoreType.DMA((2,)),
            pltpu.SemaphoreType.DMA((2,)),
            pltpu.SemaphoreType.DMA((17,)),
            pltpu.SemaphoreType.DMA((17,)),
            pltpu.SemaphoreType.DMA((16,)),
            pltpu.SemaphoreType.DMA((16,)),
        ],
        compiler_params=pltpu.CompilerParams(
            collective_id=0, has_side_effects=True, vmem_limit_bytes=56 * 1024 * 1024
        ),
    )(tokens, quant_weight, block_scales.reshape(1, -1), key_grad)


def solution(mesh):
    paired = mesh.shape["rep"] == 8 and mesh.shape["fsdp"] == 4
    return jax.shard_map(
        fused_body if paired else body,
        mesh=mesh,
        in_specs=(P(("rep", "fsdp"), None), P("fsdp", None), P("fsdp"), P(("rep", "fsdp"), None)),
        out_specs=(P(("rep", "fsdp"), None), P(("rep", "fsdp"), None), P(("rep", "fsdp"), None)),
        check_vma=False,
    )
```

time: 49.5 us -> 50 us (1.010)
  Pallas kernels: 42 us -> 42.9 us
    unnamed x9 -> x5, local copies, waits for them, and re-layouts: 6.03 us -> 5.01 us
    pallas_call x1, Pallas kernels: 42 us -> 42.9 us  [fused_body(): pl.pallas_call(fused_kernel, out_shape=[jax.ShapeDtypeStruct((row_count,...]
    reshape x1, local copies, waits for them, and re-layouts: 0.66 us -> 1.22 us  [fused_body(): block_scales.reshape(1, -1)]
where the time goes in v2:
time: 50 us; the launch traced here: 49.8 us
  Pallas kernels  42.9 us (86%)
  local copies, waits for them, and re-layouts  6.23 us (12%)
  between operations  0.64 us (1%)
    pallas_call x1, Pallas kernels, fused_body(): pl.pallas_call(fused_kernel, out_shape=[jax.ShapeDtypeStruct((row_count,...  42.9 us
    unnamed x5, local copies, waits for them, and re-layouts  5.01 us
    reshape x1, local copies, waits for them, and re-layouts, fused_body(): block_scales.reshape(1, -1)  1.22 us

profile of v2, /device:TPU:0, one launch (start us, length us, event | category | flops | bytes accessed | tf_op | source)
XLA Modules:
  0.0 49.8 jit_solution(16534990566541387586)
XLA Ops:
  0.6 1.2 %reshape.9.scale_ref = bf16[1,256]{1,0:T(2,128)(2,1)} reshape(bf16[256]{0:T(256)(128)(2,1)} %param.6) | data formatting | bytes 1024 | tf_op jit(solution)/shard_map/reshape | solution.py:403
  1.9 42.9 %shard_map.67 = (bf16[192,512]{1,0:T(8,128)(2,1)}, bf16[192,4096]{1,0:T(8,128)(2,1)}, bf16[128,512]{1,0:T(8,128)(2,1)}) custom-call(bf16[192,4096]{1,0:T(8,128)(2,1)} %tok_hbm.1, bf16[1024,512]{1,0:T(8,128)(2,1)} %quant_hbm.1, bf16[1,256]{1,0:T(2,128)(2,1)} %reshape.9.scale_ref, bf16[192,512]{1,0:T(8,128)(2,1)} %kg_hbm.1), custom_call_target="tpu_custom_call" | custom-call | tf_op jit(solution)/shard_map/pallas_call | solution.py:370
  44.7 1.6 %copy.10 = bf16[192,512]{1,0:T(8,128)(2,1)} copy(bf16[192,512]{1,0:T(8,128)(2,1)} %get-tuple-element.6) | data formatting | bytes 393216
  46.4 0.0 copy-start
  46.4 2.7 %copy.11 = bf16[192,4096]{1,0:T(8,128)(2,1)} copy(bf16[192,4096]{1,0:T(8,128)(2,1)} %get-tuple-element.7) | data formatting | bytes 3145728
  49.1 0.0 copy-done
  49.1 0.7 %copy.12 = bf16[128,512]{1,0:T(8,128)(2,1)} copy(bf16[128,512]{1,0:T(8,128)(2,1)S(1)} %copy-done) | data formatting | bytes 262144
Async XLA Ops:
  46.4 2.7 %copy-start = (bf16[128,512]{1,0:T(8,128)(2,1)S(1)}, bf16[128,512]{1,0:T(8,128)(2,1)}, u32[]{:S(2)}) copy-start(bf16[128,512]{1,0:T(8,128)(2,1)} %get-tuple-element.8) | copy-start | bytes 393220

commit v3 on v2

--- a/solution.py
+++ b/solution.py
@@ -90,7 +90,7 @@
     rot_ref, tg_hbm, wg_ref,
     tok_ref, quant_ref, kg_ref, tg_ref,
     wbuf, tok_twin, pg, proj, cos_t, sin_t,
-    s_a, s_b, a1, b1, a2, b2, a3, b3, a4, b4,
+    sa, sb, sc, sd, a1, b1, c1, d1, a2, b2, c2, d2, a3, b3, c3, d3, a4, b4, c4, d4,
     load_sem, store_sem, tok_sem, pg_sem, w_send, w_recv, rs_send, rs_recv,
 ):
     rep, fsdp = lax.axis_index("rep"), lax.axis_index("fsdp")
@@ -167,16 +167,28 @@
         device_id=twin, device_id_type=MESH,
     )
 
-    shape = (row_count, HEAD_DIM)
     half = HEAD_DIM // 2
-    lane = lax.broadcasted_iota(jnp.int32, shape, 1)
-    steps = (lane % half).astype(jnp.float32)
-    frequency = jnp.exp(steps * (-2.0 * math.log(rope_base) / HEAD_DIM))
-    place = (fsdp * row_count + lax.broadcasted_iota(jnp.int32, shape, 0)).astype(jnp.float32)
-    angles = place * frequency
-    cos_t[...] = jnp.cos(angles)
-    sine = jnp.sin(angles)
-    sin_t[...] = jnp.where(lane < half, -sine, sine)
+    low_rows = 8
+    high_rows = row_count // low_rows
+
+    def angles(rows, first, step):
+        shape = (rows, HEAD_DIM)
+        steps = (lax.broadcasted_iota(jnp.int32, shape, 1) % half).astype(jnp.float32)
+        frequency = jnp.exp(steps * (-2.0 * math.log(rope_base) / HEAD_DIM))
+        place = first + step * lax.broadcasted_iota(jnp.int32, shape, 0)
+        return place.astype(jnp.float32) * frequency
+
+    high = angles(high_rows, fsdp * row_count, low_rows)
+    low = angles(low_rows, 0, 1)
+    cos_high, sin_high = jnp.cos(high), jnp.sin(high)
+    cos_low, sin_low = jnp.cos(low), jnp.sin(low)
+    leading = lax.broadcasted_iota(jnp.int32, (low_rows, HEAD_DIM), 1) < half
+    for i in range(high_rows):
+        rows = slice(i * low_rows, (i + 1) * low_rows)
+        ch, sh = cos_high[i : i + 1], sin_high[i : i + 1]
+        cos_t[rows, :] = ch * cos_low - sh * sin_low
+        sine = sh * cos_low + ch * sin_low
+        sin_t[rows, :] = jnp.where(leading, -sine, sine)
 
     def turn(value, direction):
         return value * cos_t[...] + pltpu.roll(value, half, 1) * (direction * sin_t[...])
@@ -188,16 +200,11 @@
         pg[0, :, cols] = turn(kg_ref[:, cols].astype(jnp.float32), -1.0).astype(jnp.bfloat16)
     pg_copy = send(pg.at[0], pg.at[1], pg_sem.at[0], pg_sem.at[1], twin)
 
-    def dequant_other(i, carry):
-        other = (2 * here + 2 + i) % 8
-        dequant(other)
-        return carry
-
-    lax.fori_loop(0, 6, dequant_other, 0)
     load_tok.wait()
     all_tokens.wait_recv()
     pg_copy.wait_recv()
-    own = send(wbuf.at[fsdp], wbuf.at[fsdp], w_send.at[16], w_recv.at[16], twin)
+
+    quarter = block // 4
 
     def blocks(bx, by):
         def one(bz, carry):
@@ -209,8 +216,10 @@
             total = lax.dot_general(
                 left, right, (((0,), (0,)), ((), ())), preferred_element_type=jnp.float32
             ).astype(jnp.bfloat16)
-            s_a[bx, by, bz0, bz1] = total[: block // 2]
-            s_b[by, bx, bz0, bz1] = total[block // 2 :]
+            sa[bx, by, bz0, bz1] = total[:quarter]
+            sb[by, bx, bz0, bz1] = total[quarter : 2 * quarter]
+            sc[bx, by, bz0, bz1] = total[2 * quarter : 3 * quarter]
+            sd[by, bx, bz0, bz1] = total[3 * quarter :]
             return carry
 
         lax.fori_loop(0, 4, one, 0)
@@ -252,8 +261,12 @@
             count = row_count * lax.axis_size("rep") * lax.axis_size("fsdp")
             wg_ref[rows, :] = (total * (1.0 / math.sqrt(count))).astype(jnp.bfloat16)
 
-    fa = Flow(0, (x, y, z0, z1), (over_x, over_y, over_z0, over_z1), (s_a, a1, a2, a3, a4))
-    fb = Flow(1, (y, x, z0, z1), (over_y, over_x, over_z0, over_z1), (s_b, b1, b2, b3, b4))
+    x_first = ((x, y, z0, z1), (over_x, over_y, over_z0, over_z1))
+    y_first = ((y, x, z0, z1), (over_y, over_x, over_z0, over_z1))
+    fa = Flow(0, *x_first, (sa, a1, a2, a3, a4))
+    fb = Flow(1, *y_first, (sb, b1, b2, b3, b4))
+    fc = Flow(2, *x_first, (sc, c1, c2, c3, c4))
+    fd = Flow(3, *y_first, (sd, d1, d2, d3, d4))
 
     def use(shard, at):
         col = pl.multiple_of(shard * shard_rows + at * piece, piece)
@@ -303,51 +316,75 @@
     pass_y(0)
     blocks(1 - x, y)
     blocks(x, 1 - y)
-    pass_y(1)
     fa.launch(0, 1)
     fb.launch(0, 1)
+    pass_y(1)
     blocks(x, y)
+    def dequant_other(i, carry):
+        other = (2 * here + 2 + i) % 8
+        dequant(other)
+        return carry
+
+    lax.fori_loop(0, 6, dequant_other, 0)
+    own = send(wbuf.at[fsdp], wbuf.at[fsdp], w_send.at[16], w_recv.at[16], twin)
     use_all(fsdp)
     pass_x(0)
+    fa.take(0, 0)
+    fb.take(0, 0)
+    for turn_of in range(2):
+        fc.launch(0, turn_of)
+        fd.launch(0, turn_of)
+    pass_z(0)
+    pass_x(1)
     own.wait_recv()
     use(twin_shard, 0)
     use(twin_shard, 1)
-    pass_z(0)
+    pass_z(1)
+    fa.take(0, 1)
+    fb.take(0, 1)
     use(twin_shard, 2)
     use(twin_shard, 3)
-    pass_x(1)
-    pass_z(1)
-    fa.take(0, 0)
-    fb.take(0, 0)
+    fa.take(1, 0)
+    fb.take(1, 0)
     use(side, here)
     pass_z(2)
+    fc.take(0, 0)
+    fd.take(0, 0)
+    fa.take(1, 1)
+    fb.take(1, 1)
+    pass_z(3)
     use(side, there_x)
     use(side, there_z)
-    fb.take(0, 1)
-    fa.take(0, 1)
-    pass_z(3)
-    fa.take(1, 0)
-    fb.take(1, 0)
+    fa.take(2, 0)
+    fb.take(2, 0)
+    fc.take(0, 1)
+    fd.take(0, 1)
     use(side, there)
     for copy in from_twin[:2]:
         copy.wait_recv()
     use(twin_side, here)
-    fa.take(1, 1)
-    fb.take(1, 1)
-    fa.take(2, 0)
-    fb.take(2, 0)
+    fc.take(1, 0)
+    fd.take(1, 0)
+    fa.take(2, 1)
+    fb.take(2, 1)
     for copy in from_twin[2:]:
         copy.wait_recv()
     use(twin_side, there_x)
     use(twin_side, there_z)
-    fa.take(2, 1)
-    fb.take(2, 1)
+    fc.take(1, 1)
+    fd.take(1, 1)
     use(twin_side, there)
+    fc.take(2, 0)
+    fd.take(2, 0)
     for h in range(heads):
         cols = slice(h * HEAD_DIM, (h + 1) * HEAD_DIM)
         rot_ref[:, cols] = turn(proj[:, cols], 1.0).astype(jnp.bfloat16)
-    fa.finish(slice(0, block // 2))
-    fb.finish(slice(block // 2, block))
+    fa.finish(slice(0, quarter))
+    fb.finish(slice(quarter, 2 * quarter))
+    fc.take(2, 1)
+    fd.take(2, 1)
+    fc.finish(slice(2 * quarter, 3 * quarter))
+    fd.finish(slice(3 * quarter, block))
 
     pltpu.make_async_copy(tg_ref, tg_hbm, store_sem.at[0]).wait()
     all_tokens.wait_send()
@@ -363,11 +400,11 @@
     vmem = pl.BlockSpec(memory_space=pltpu.VMEM)
     hbm = pl.BlockSpec(memory_space=pltpu.HBM)
     flows = [
-        pltpu.VMEM((2,) * (4 - level) + (block // 2, width), bf16)
+        pltpu.VMEM((2,) * (4 - level) + (block // 4, width), bf16)
         for level in range(5)
-        for _ in range(2)
+        for _ in range(4)
     ]
-    return pl.pallas_call(
+    results = pl.pallas_call(
         fused_kernel,
         out_shape=[
             jax.ShapeDtypeStruct((row_count, width), bf16),
@@ -394,13 +431,36 @@
             pltpu.SemaphoreType.DMA((2,)),
             pltpu.SemaphoreType.DMA((17,)),
             pltpu.SemaphoreType.DMA((17,)),
-            pltpu.SemaphoreType.DMA((16,)),
-            pltpu.SemaphoreType.DMA((16,)),
+            pltpu.SemaphoreType.DMA((32,)),
+            pltpu.SemaphoreType.DMA((32,)),
         ],
         compiler_params=pltpu.CompilerParams(
             collective_id=0, has_side_effects=True, vmem_limit_bytes=56 * 1024 * 1024
         ),
     )(tokens, quant_weight, block_scales.reshape(1, -1), key_grad)
+    return pl.pallas_call(
+        place_kernel,
+        out_shape=[jax.ShapeDtypeStruct(value.shape, value.dtype) for value in results],
+        in_specs=[hbm] * 3,
+        out_specs=[hbm] * 3,
+        scratch_shapes=[pltpu.SemaphoreType.DMA((6,))],
+    )(*results)
+
+
+def place_kernel(rot_in, tg_in, wg_in, rot_out, tg_out, wg_out, sems):
+    rows = tg_in.shape[0] // 4
+    copies = [
+        pltpu.make_async_copy(
+            tg_in.at[pl.ds(i * rows, rows)], tg_out.at[pl.ds(i * rows, rows)], sems.at[i]
+        )
+        for i in range(4)
+    ]
+    copies.append(pltpu.make_async_copy(rot_in, rot_out, sems.at[4]))
+    copies.append(pltpu.make_async_copy(wg_in, wg_out, sems.at[5]))
+    for copy in copies:
+        copy.start()
+    for copy in copies:
+        copy.wait()
 
 
 def solution(mesh):

time: 50 us -> 103 us (2.06)
  Pallas kernels: 42.9 us -> 101 us
  local copies, waits for them, and re-layouts: 6.23 us -> 1.22 us
    pallas_call x0 -> x1, Pallas kernels: none -> 58.7 us  [fused_body(): pl.pallas_call(place_kernel, out_shape=[jax.ShapeDtypeStruct(value.shape,...]
    unnamed x5 -> x0, local copies, waits for them, and re-layouts: 5.01 us -> none
where the time goes in v3:
time: 103 us
  Pallas kernels  101 us (98%)
  local copies, waits for them, and re-layouts  1.22 us (1%)
    pallas_call x1, Pallas kernels, fused_body(): pl.pallas_call(place_kernel, out_shape=[jax.ShapeDtypeStruct(value.shape,...  58.7 us
    pallas_call x1, Pallas kernels, fused_body(): pl.pallas_call(fused_kernel, out_shape=[jax.ShapeDtypeStruct((row_count,...  42 us

profile of v3, /device:TPU:0, one launch (start us, length us, event | category | flops | bytes accessed | tf_op | source)
XLA Modules:
  0.0 102.6 jit_solution(6152773506293484724)
XLA Ops:
  0.6 1.2 %reshape.9.scale_ref = bf16[1,256]{1,0:T(2,128)(2,1)} reshape(bf16[256]{0:T(256)(128)(2,1)} %param.6) | data formatting | bytes 1024 | tf_op jit(solution)/shard_map/reshape | solution.py:440
  1.9 42.0 %shard_map.67 = (bf16[192,512]{1,0:T(8,128)(2,1)}, bf16[192,4096]{1,0:T(8,128)(2,1)}, bf16[128,512]{1,0:T(8,128)(2,1)}) custom-call(bf16[192,4096]{1,0:T(8,128)(2,1)} %tok_hbm.1, bf16[1024,512]{1,0:T(8,128)(2,1)} %quant_hbm.1, bf16[1,256]{1,0:T(2,128)(2,1)} %reshape.9.scale_ref, bf16[192,512]{1,0:T(8,128)(2,1)} %kg_hbm.1), custom_call_target="tpu_custom_call" | custom-call | tf_op jit(solution)/shard_map/pallas_call | solution.py:407
  43.8 58.7 %shard_map.68 = (bf16[192,512]{1,0:T(8,128)(2,1)}, bf16[192,4096]{1,0:T(8,128)(2,1)}, bf16[128,512]{1,0:T(8,128)(2,1)}) custom-call(bf16[192,512]{1,0:T(8,128)(2,1)} %get-tuple-element.6.rot_in, bf16[192,4096]{1,0:T(8,128)(2,1)} %get-tuple-element.7.tg_in, bf16[128,512]{1,0:T(8,128)(2,1)} %get-tuple-element.8.wg_in), custom_call_target="tpu_custom_call" | custom-call | tf_op jit(solution)/shard_map/pallas_call | solution.py:441

commit v4 on v3

--- a/solution.py
+++ b/solution.py
@@ -87,11 +87,11 @@
 
 def fused_kernel(
     tok_hbm, quant_hbm, scale_ref, kg_hbm,
-    rot_ref, tg_hbm, wg_ref,
-    tok_ref, quant_ref, kg_ref, tg_ref,
+    rot_ref, tg_ref, wg_ref,
+    tok_ref, quant_ref, kg_ref,
     wbuf, tok_twin, pg, proj, cos_t, sin_t,
     sa, sb, sc, sd, a1, b1, c1, d1, a2, b2, c2, d2, a3, b3, c3, d3, a4, b4, c4, d4,
-    load_sem, store_sem, tok_sem, pg_sem, w_send, w_recv, rs_send, rs_recv,
+    load_sem, tok_sem, pg_sem, w_send, w_recv, rs_send, rs_recv,
 ):
     rep, fsdp = lax.axis_index("rep"), lax.axis_index("fsdp")
     x, z0, z1 = rep % 2, (rep // 2) % 2, rep // 4
@@ -121,51 +121,13 @@
 
     def dequant(i):
         rows = pl.ds(pl.multiple_of(i * part, part), part)
-        n_blocks = scale_ref.shape[1]
+        n_blocks = scale_ref.shape[0]
         per_block = shard_rows // n_blocks
         owner = (i * part + lax.broadcasted_iota(jnp.int32, (part, n_blocks), 0)) // per_block
         lane = lax.broadcasted_iota(jnp.int32, (part, n_blocks), 1)
-        picked = jnp.where(owner == lane, scale_ref[...].astype(jnp.float32), 0.0)
+        picked = jnp.where(owner == lane, scale_ref[...].astype(jnp.float32).reshape(1, n_blocks), 0.0)
         column = jnp.sum(picked, axis=1, keepdims=True)
         wbuf[fsdp, i] = (quant_ref[rows, :].astype(jnp.float32) * column).astype(jnp.bfloat16)
-
-    load_quant.wait()
-    dequant(2 * here)
-    dequant(2 * here + 1)
-    pl.semaphore_wait(barrier, 5)
-
-    started = []
-
-    def send(src, dst, send_sem, recv_sem, to):
-        copy = pltpu.make_async_remote_copy(
-            src_ref=src, dst_ref=dst, send_sem=send_sem, recv_sem=recv_sem,
-            device_id=to, device_id_type=MESH,
-        )
-        copy.start()
-        started.append(copy)
-        return copy
-
-    def send_w(shard, i, slot, to):
-        return send(
-            wbuf.at[shard, i], wbuf.at[shard, i], w_send.at[slot], w_recv.at[slot], to
-        )
-
-    from_y = [send_w(fsdp, 2 * here + q, q, over_y) for q in range(2)]
-
-    def send_tokens(j, carry):
-        col = pl.multiple_of((2 * j + 1 - c) * block, block)
-        pltpu.make_async_remote_copy(
-            src_ref=tok_hbm.at[:, pl.ds(col, block)], dst_ref=tok_twin.at[j],
-            send_sem=tok_sem.at[0], recv_sem=tok_sem.at[1],
-            device_id=twin, device_id_type=MESH,
-        ).start()
-        return carry
-
-    lax.fori_loop(0, 16, send_tokens, 0)
-    all_tokens = pltpu.make_async_remote_copy(
-        src_ref=tok_twin, dst_ref=tok_twin, send_sem=tok_sem.at[0], recv_sem=tok_sem.at[1],
-        device_id=twin, device_id_type=MESH,
-    )
 
     half = HEAD_DIM // 2
     low_rows = 8
@@ -198,31 +160,76 @@
     for h in range(heads):
         cols = slice(h * HEAD_DIM, (h + 1) * HEAD_DIM)
         pg[0, :, cols] = turn(kg_ref[:, cols].astype(jnp.float32), -1.0).astype(jnp.bfloat16)
+    load_quant.wait()
+    dequant(2 * here)
+    dequant(2 * here + 1)
+    pl.semaphore_wait(barrier, 5)
+
+    started = []
+
+    def send(src, dst, send_sem, recv_sem, to):
+        copy = pltpu.make_async_remote_copy(
+            src_ref=src, dst_ref=dst, send_sem=send_sem, recv_sem=recv_sem,
+            device_id=to, device_id_type=MESH,
+        )
+        copy.start()
+        started.append(copy)
+        return copy
+
+    def send_w(shard, i, slot, to):
+        return send(
+            wbuf.at[shard, i], wbuf.at[shard, i], w_send.at[slot], w_recv.at[slot], to
+        )
+
+    from_y = [send_w(fsdp, 2 * here + q, q, over_y) for q in range(2)]
+
+    def send_tokens(bx, by):
+        group = 2 * bx + by
+        for k in range(4):
+            col = pl.multiple_of(((k % 2 * 8 + k // 2 * 4 + group) * 2 + 1 - c) * block, block)
+            pltpu.make_async_remote_copy(
+                src_ref=tok_ref.at[:, pl.ds(col, block)],
+                dst_ref=tok_twin.at[bx, by, :, pl.ds(k * block, block)],
+                send_sem=tok_sem.at[group], recv_sem=tok_sem.at[4 + group],
+                device_id=twin, device_id_type=MESH,
+            ).start()
+
+    def group_copy(bx, by):
+        group = 2 * bx + by
+        return pltpu.make_async_remote_copy(
+            src_ref=tok_twin.at[bx, by], dst_ref=tok_twin.at[bx, by],
+            send_sem=tok_sem.at[group], recv_sem=tok_sem.at[4 + group],
+            device_id=twin, device_id_type=MESH,
+        )
+
+    load_tok.wait()
+    send_tokens(1 - x, 1 - y)
     pg_copy = send(pg.at[0], pg.at[1], pg_sem.at[0], pg_sem.at[1], twin)
-
-    load_tok.wait()
-    all_tokens.wait_recv()
+    send_tokens(1 - x, y)
+    send_tokens(x, 1 - y)
+    send_tokens(x, y)
     pg_copy.wait_recv()
 
     quarter = block // 4
 
     def blocks(bx, by):
-        def one(bz, carry):
-            bz0, bz1 = bz // 2, bz % 2
-            index = bz1 * 8 + bz0 * 4 + bx * 2 + by
-            col = pl.multiple_of((2 * index + c) * block, block)
-            left = jnp.concatenate([tok_ref[:, pl.ds(col, block)], tok_twin[index]], axis=0)
-            right = pg[...].reshape(2 * row_count, width)
-            total = lax.dot_general(
-                left, right, (((0,), (0,)), ((), ())), preferred_element_type=jnp.float32
-            ).astype(jnp.bfloat16)
-            sa[bx, by, bz0, bz1] = total[:quarter]
-            sb[by, bx, bz0, bz1] = total[quarter : 2 * quarter]
-            sc[bx, by, bz0, bz1] = total[2 * quarter : 3 * quarter]
-            sd[by, bx, bz0, bz1] = total[3 * quarter :]
-            return carry
-
-        lax.fori_loop(0, 4, one, 0)
+        group_copy(bx, by).wait_recv()
+        own_columns = [
+            tok_ref[:, pl.ds(pl.multiple_of(((k % 2 * 8 + k // 2 * 4 + 2 * bx + by) * 2 + c) * block, block), block)]
+            for k in range(4)
+        ]
+        left = jnp.concatenate(
+            [jnp.concatenate(own_columns, axis=1), tok_twin[bx, by]], axis=0
+        )
+        right = pg[...].reshape(2 * row_count, width)
+        total = lax.dot_general(
+            left, right, (((0,), (0,)), ((), ())), preferred_element_type=jnp.float32
+        ).astype(jnp.bfloat16).reshape(2, 2, 4, quarter, width)
+        sa[bx, by] = total[:, :, 0]
+        sb[by, bx] = total[:, :, 1]
+        for bz0 in range(2):
+            sc[bx, bz0, by] = total[bz0, :, 2]
+            sd[by, bz0, bx] = total[bz0, :, 3]
 
     class Flow:
         def __init__(self, index, bits, others, bufs):
@@ -265,8 +272,10 @@
     y_first = ((y, x, z0, z1), (over_y, over_x, over_z0, over_z1))
     fa = Flow(0, *x_first, (sa, a1, a2, a3, a4))
     fb = Flow(1, *y_first, (sb, b1, b2, b3, b4))
-    fc = Flow(2, *x_first, (sc, c1, c2, c3, c4))
-    fd = Flow(3, *y_first, (sd, d1, d2, d3, d4))
+    x_then_z = ((x, z0, y, z1), (over_x, over_z0, over_y, over_z1))
+    y_then_z = ((y, z0, x, z1), (over_y, over_z0, over_x, over_z1))
+    fc = Flow(2, *x_then_z, (sc, c1, c2, c3, c4))
+    fd = Flow(3, *y_then_z, (sd, d1, d2, d3, d4))
 
     def use(shard, at):
         col = pl.multiple_of(shard * shard_rows + at * piece, piece)
@@ -275,7 +284,6 @@
         tg_ref[:, cols] = lax.dot_general(
             pg[0], w, (((1,), (1,)), ((), ())), preferred_element_type=jnp.float32
         ).astype(jnp.bfloat16)
-        pltpu.make_async_copy(tg_ref.at[:, cols], tg_hbm.at[:, cols], store_sem.at[0]).start()
         proj[...] += jnp.dot(tok_ref[:, cols], w, preferred_element_type=jnp.float32)
 
     def use_all(shard):
@@ -386,8 +394,8 @@
     fc.finish(slice(2 * quarter, 3 * quarter))
     fd.finish(slice(3 * quarter, block))
 
-    pltpu.make_async_copy(tg_ref, tg_hbm, store_sem.at[0]).wait()
-    all_tokens.wait_send()
+    for group in range(4):
+        group_copy(group // 2, group % 2).wait_send()
     for copy in started:
         copy.wait_send()
 
@@ -407,27 +415,25 @@
     results = pl.pallas_call(
         fused_kernel,
         out_shape=[
-            jax.ShapeDtypeStruct((row_count, width), bf16),
-            jax.ShapeDtypeStruct((row_count, model), bf16),
-            jax.ShapeDtypeStruct((block, width), bf16),
+            pltpu.VMEM((row_count, width), bf16),
+            pltpu.VMEM((row_count, model), bf16),
+            pltpu.VMEM((block, width), bf16),
         ],
         in_specs=[hbm, hbm, vmem, hbm],
-        out_specs=[vmem, hbm, vmem],
+        out_specs=[vmem] * 3,
         scratch_shapes=[
             pltpu.VMEM((row_count, model), bf16),
             pltpu.VMEM((shard_rows, width), bf16),
             pltpu.VMEM((row_count, width), bf16),
-            pltpu.VMEM((row_count, model), bf16),
             pltpu.VMEM((4, 8, shard_rows // 8, width), bf16),
-            pltpu.VMEM((16, row_count, block), bf16),
+            pltpu.VMEM((2, 2, row_count, 4 * block), bf16),
             pltpu.VMEM((2, row_count, width), bf16),
             pltpu.VMEM((row_count, width), f32),
             pltpu.VMEM((row_count, HEAD_DIM), f32),
             pltpu.VMEM((row_count, HEAD_DIM), f32),
             *flows,
             pltpu.SemaphoreType.DMA((3,)),
-            pltpu.SemaphoreType.DMA((1,)),
-            pltpu.SemaphoreType.DMA((2,)),
+            pltpu.SemaphoreType.DMA((8,)),
             pltpu.SemaphoreType.DMA((2,)),
             pltpu.SemaphoreType.DMA((17,)),
             pltpu.SemaphoreType.DMA((17,)),
@@ -437,26 +443,22 @@
         compiler_params=pltpu.CompilerParams(
             collective_id=0, has_side_effects=True, vmem_limit_bytes=56 * 1024 * 1024
         ),
-    )(tokens, quant_weight, block_scales.reshape(1, -1), key_grad)
+    )(tokens, quant_weight, block_scales, key_grad)
     return pl.pallas_call(
         place_kernel,
         out_shape=[jax.ShapeDtypeStruct(value.shape, value.dtype) for value in results],
-        in_specs=[hbm] * 3,
+        in_specs=[vmem] * 3,
         out_specs=[hbm] * 3,
-        scratch_shapes=[pltpu.SemaphoreType.DMA((6,))],
+        scratch_shapes=[pltpu.SemaphoreType.DMA((3,))],
     )(*results)
 
 
 def place_kernel(rot_in, tg_in, wg_in, rot_out, tg_out, wg_out, sems):
-    rows = tg_in.shape[0] // 4
+    pairs = ((tg_in, tg_out), (rot_in, rot_out), (wg_in, wg_out))
     copies = [
-        pltpu.make_async_copy(
-            tg_in.at[pl.ds(i * rows, rows)], tg_out.at[pl.ds(i * rows, rows)], sems.at[i]
-        )
-        for i in range(4)
+        pltpu.make_async_copy(source, target, sems.at[i])
+        for i, (source, target) in enumerate(pairs)
     ]
-    copies.append(pltpu.make_async_copy(rot_in, rot_out, sems.at[4]))
-    copies.append(pltpu.make_async_copy(wg_in, wg_out, sems.at[5]))
     for copy in copies:
         copy.start()
     for copy in copies:

time: 103 us -> 46.6 us (0.45)
  Pallas kernels: 101 us -> 43.3 us
  local copies, waits for them, and re-layouts: 1.22 us -> 2.47 us
    pallas_call x1, Pallas kernels: 58.7 us -> 2.7 us  [fused_body(): pl.pallas_call(place_kernel, out_shape=[jax.ShapeDtypeStruct(value.shape,...]
    unnamed x0 -> x6, local copies, waits for them, and re-layouts: none -> 2.47 us
    pallas_call x1, Pallas kernels: 42 us -> 40.6 us  [fused_body(): pl.pallas_call(fused_kernel, out_shape=[pltpu.VMEM((row_count, width), bf...]
    reshape x1 -> x0, local copies, waits for them, and re-layouts: 1.22 us -> none  [fused_body(): block_scales.reshape(1, -1)]
where the time goes in v4:
time: 46.6 us; the launch traced here: 46.4 us
  Pallas kernels  43.3 us (93%)
  local copies, waits for them, and re-layouts  2.47 us (5%)
  between operations  0.65 us (1%)
    pallas_call x1, Pallas kernels, fused_body(): pl.pallas_call(fused_kernel, out_shape=[pltpu.VMEM((row_count, width), bf...  40.6 us
    pallas_call x1, Pallas kernels, fused_body(): pl.pallas_call(place_kernel, out_shape=[jax.ShapeDtypeStruct(value.shape,...  2.7 us
    unnamed x6, local copies, waits for them, and re-layouts  2.47 us

profile of v4, /device:TPU:0, one launch (start us, length us, event | category | flops | bytes accessed | tf_op | source)
XLA Modules:
  0.0 46.4 jit_solution(14800235395863686242)
XLA Ops:
  0.6 40.6 %shard_map.67 = (bf16[192,512]{1,0:T(8,128)(2,1)S(1)}, bf16[192,4096]{1,0:T(8,128)(2,1)S(1)}, bf16[128,512]{1,0:T(8,128)(2,1)S(1)}) custom-call(bf16[192,4096]{1,0:T(8,128)(2,1)} %tok_hbm.1, bf16[1024,512]{1,0:T(8,128)(2,1)} %quant_hbm.1, bf16[256]{0:T(256)(128)(2,1)} %scale_ref.1, bf16[192,512]{1,0:T(8,128)(2,1)} %kg_hbm.1), custom_call_target="tpu_custom_call" | custom-call | tf_op jit(solution)/shard_map/pallas_call | solution.py:415
  41.2 0.0 copy-start
  41.2 1.2 %copy-done = bf16[192,4096]{1,0:T(8,128)(2,1)} copy-done((bf16[192,4096]{1,0:T(8,128)(2,1)}, bf16[192,4096]{1,0:T(8,128)(2,1)S(1)}, u32[]{:S(2)}) %copy-start) | copy-done | bytes 1572888
  42.4 0.0 copy-start.1
  42.4 0.7 %copy-done.1 = bf16[192,512]{1,0:T(8,128)(2,1)} copy-done((bf16[192,512]{1,0:T(8,128)(2,1)}, bf16[192,512]{1,0:T(8,128)(2,1)S(1)}, u32[]{:S(2)}) %copy-start.1) | copy-done | bytes 196632
  43.1 0.0 copy-start.2
  43.1 0.6 %copy-done.2 = bf16[128,512]{1,0:T(8,128)(2,1)} copy-done((bf16[128,512]{1,0:T(8,128)(2,1)}, bf16[128,512]{1,0:T(8,128)(2,1)S(1)}, u32[]{:S(2)}) %copy-start.2) | copy-done | bytes 131096
  43.7 2.7 %shard_map.68 = (bf16[192,512]{1,0:T(8,128)(2,1)}, bf16[192,4096]{1,0:T(8,128)(2,1)}, bf16[128,512]{1,0:T(8,128)(2,1)}) custom-call(bf16[192,512]{1,0:T(8,128)(2,1)} %copy-done.1, bf16[192,4096]{1,0:T(8,128)(2,1)} %copy-done, bf16[128,512]{1,0:T(8,128)(2,1)} %copy-done.2), custom_call_target="tpu_custom_call" | custom-call | tf_op jit(solution)/shard_map/pallas_call | solution.py:447
Async XLA Ops:
  41.2 1.2 %copy-start = (bf16[192,4096]{1,0:T(8,128)(2,1)}, bf16[192,4096]{1,0:T(8,128)(2,1)S(1)}, u32[]{:S(2)}) copy-start(bf16[192,4096]{1,0:T(8,128)(2,1)S(1)} %get-tuple-element.7.tg_in) | copy-start | bytes 4718596
  42.4 0.7 %copy-start.1 = (bf16[192,512]{1,0:T(8,128)(2,1)}, bf16[192,512]{1,0:T(8,128)(2,1)S(1)}, u32[]{:S(2)}) copy-start(bf16[192,512]{1,0:T(8,128)(2,1)S(1)} %get-tuple-element.6.rot_in) | copy-start | bytes 589828
  43.1 0.6 %copy-start.2 = (bf16[128,512]{1,0:T(8,128)(2,1)}, bf16[128,512]{1,0:T(8,128)(2,1)S(1)}, u32[]{:S(2)}) copy-start(bf16[128,512]{1,0:T(8,128)(2,1)S(1)} %get-tuple-element.8.wg_in) | copy-start | bytes 393220

commit v5 on v4

--- a/solution.py
+++ b/solution.py
@@ -88,7 +88,7 @@
 def fused_kernel(
     tok_hbm, quant_hbm, scale_ref, kg_hbm,
     rot_ref, tg_ref, wg_ref,
-    tok_ref, quant_ref, kg_ref,
+    tok_ref, quant_ref, kg_ref, kg_twin,
     wbuf, tok_twin, pg, proj, cos_t, sin_t,
     sa, sb, sc, sd, a1, b1, c1, d1, a2, b2, c2, d2, a3, b3, c3, d3, a4, b4, c4, d4,
     load_sem, tok_sem, pg_sem, w_send, w_recv, rs_send, rs_recv,
@@ -129,37 +129,6 @@
         column = jnp.sum(picked, axis=1, keepdims=True)
         wbuf[fsdp, i] = (quant_ref[rows, :].astype(jnp.float32) * column).astype(jnp.bfloat16)
 
-    half = HEAD_DIM // 2
-    low_rows = 8
-    high_rows = row_count // low_rows
-
-    def angles(rows, first, step):
-        shape = (rows, HEAD_DIM)
-        steps = (lax.broadcasted_iota(jnp.int32, shape, 1) % half).astype(jnp.float32)
-        frequency = jnp.exp(steps * (-2.0 * math.log(rope_base) / HEAD_DIM))
-        place = first + step * lax.broadcasted_iota(jnp.int32, shape, 0)
-        return place.astype(jnp.float32) * frequency
-
-    high = angles(high_rows, fsdp * row_count, low_rows)
-    low = angles(low_rows, 0, 1)
-    cos_high, sin_high = jnp.cos(high), jnp.sin(high)
-    cos_low, sin_low = jnp.cos(low), jnp.sin(low)
-    leading = lax.broadcasted_iota(jnp.int32, (low_rows, HEAD_DIM), 1) < half
-    for i in range(high_rows):
-        rows = slice(i * low_rows, (i + 1) * low_rows)
-        ch, sh = cos_high[i : i + 1], sin_high[i : i + 1]
-        cos_t[rows, :] = ch * cos_low - sh * sin_low
-        sine = sh * cos_low + ch * sin_low
-        sin_t[rows, :] = jnp.where(leading, -sine, sine)
-
-    def turn(value, direction):
-        return value * cos_t[...] + pltpu.roll(value, half, 1) * (direction * sin_t[...])
-
-    heads = width // HEAD_DIM
-    load_kg.wait()
-    for h in range(heads):
-        cols = slice(h * HEAD_DIM, (h + 1) * HEAD_DIM)
-        pg[0, :, cols] = turn(kg_ref[:, cols].astype(jnp.float32), -1.0).astype(jnp.bfloat16)
     load_quant.wait()
     dequant(2 * here)
     dequant(2 * here + 1)
@@ -202,13 +171,51 @@
             device_id=twin, device_id_type=MESH,
         )
 
+    load_kg.wait()
+    kg_copy = send(kg_ref, kg_twin, pg_sem.at[0], pg_sem.at[1], twin)
     load_tok.wait()
     send_tokens(1 - x, 1 - y)
-    pg_copy = send(pg.at[0], pg.at[1], pg_sem.at[0], pg_sem.at[1], twin)
     send_tokens(1 - x, y)
     send_tokens(x, 1 - y)
     send_tokens(x, y)
-    pg_copy.wait_recv()
+
+    half = HEAD_DIM // 2
+    low_rows = 8
+    high_rows = row_count // low_rows
+
+    def angles(rows, first, step):
+        shape = (rows, HEAD_DIM)
+        steps = (lax.broadcasted_iota(jnp.int32, shape, 1) % half).astype(jnp.float32)
+        frequency = jnp.exp(steps * (-2.0 * math.log(rope_base) / HEAD_DIM))
+        place = first + step * lax.broadcasted_iota(jnp.int32, shape, 0)
+        return place.astype(jnp.float32) * frequency
+
+    low = angles(low_rows, 0, 1)
+    cos_low, sin_low = jnp.cos(low), jnp.sin(low)
+    leading = lax.broadcasted_iota(jnp.int32, (low_rows, HEAD_DIM), 1) < half
+    heads = width // HEAD_DIM
+
+    def turn(value, whose, direction):
+        flipped = pltpu.roll(value, half, 1) * (direction * sin_t[whose])
+        return value * cos_t[whose] + flipped
+
+    def make_pg(whose, owner, source):
+        high = angles(high_rows, owner * row_count, low_rows)
+        cos_high, sin_high = jnp.cos(high), jnp.sin(high)
+        for i in range(high_rows):
+            rows = slice(i * low_rows, (i + 1) * low_rows)
+            ch, sh = cos_high[i : i + 1], sin_high[i : i + 1]
+            cos_t[whose, rows, :] = ch * cos_low - sh * sin_low
+            sine = sh * cos_low + ch * sin_low
+            sin_t[whose, rows, :] = jnp.where(leading, -sine, sine)
+        for h in range(heads):
+            cols = slice(h * HEAD_DIM, (h + 1) * HEAD_DIM)
+            value = source[:, cols].astype(jnp.float32)
+            pg[whose, :, cols] = turn(value, whose, -1.0).astype(jnp.bfloat16)
+
+    make_pg(0, fsdp, kg_ref)
+    kg_copy.wait_recv()
+    make_pg(1, fsdp + 1 - 2 * c, kg_twin)
 
     quarter = block // 4
 
@@ -386,7 +393,7 @@
     fd.take(2, 0)
     for h in range(heads):
         cols = slice(h * HEAD_DIM, (h + 1) * HEAD_DIM)
-        rot_ref[:, cols] = turn(proj[:, cols], 1.0).astype(jnp.bfloat16)
+        rot_ref[:, cols] = turn(proj[:, cols], 0, 1.0).astype(jnp.bfloat16)
     fa.finish(slice(0, quarter))
     fb.finish(slice(quarter, 2 * quarter))
     fc.take(2, 1)
@@ -425,12 +432,13 @@
             pltpu.VMEM((row_count, model), bf16),
             pltpu.VMEM((shard_rows, width), bf16),
             pltpu.VMEM((row_count, width), bf16),
+            pltpu.VMEM((row_count, width), bf16),
             pltpu.VMEM((4, 8, shard_rows // 8, width), bf16),
             pltpu.VMEM((2, 2, row_count, 4 * block), bf16),
             pltpu.VMEM((2, row_count, width), bf16),
             pltpu.VMEM((row_count, width), f32),
-            pltpu.VMEM((row_count, HEAD_DIM), f32),
-            pltpu.VMEM((row_count, HEAD_DIM), f32),
+            pltpu.VMEM((2, row_count, HEAD_DIM), f32),
+            pltpu.VMEM((2, row_count, HEAD_DIM), f32),
             *flows,
             pltpu.SemaphoreType.DMA((3,)),
             pltpu.SemaphoreType.DMA((8,)),
@@ -450,6 +458,7 @@
         in_specs=[vmem] * 3,
         out_specs=[hbm] * 3,
         scratch_shapes=[pltpu.SemaphoreType.DMA((3,))],
+        compiler_params=pltpu.CompilerParams(vmem_limit_bytes=4 * 1024 * 1024),
     )(*results)
 
 

time: 46.6 us -> 42.7 us (0.916)
  local copies, waits for them, and re-layouts: 2.47 us -> 0 us
  Pallas kernels: 43.3 us -> 41.9 us
    unnamed x6 -> x0, local copies, waits for them, and re-layouts: 2.47 us -> none
    pallas_call x1, Pallas kernels: 2.7 us -> 1.27 us  [fused_body(): pl.pallas_call(place_kernel, out_shape=[jax.ShapeDtypeStruct(value.shape,...]
where the time goes in v5:
time: 42.7 us; the launch traced here: 42.6 us
  Pallas kernels  41.9 us (98%)
  between operations  0.64 us (1%)
    pallas_call x1, Pallas kernels, fused_body(): pl.pallas_call(fused_kernel, out_shape=[pltpu.VMEM((row_count, width), bf...  40.7 us
    pallas_call x1, Pallas kernels, fused_body(): pl.pallas_call(place_kernel, out_shape=[jax.ShapeDtypeStruct(value.shape,...  1.27 us

profile of v5, /device:TPU:0, one launch (start us, length us, event | category | flops | bytes accessed | tf_op | source)
XLA Modules:
  0.0 42.6 jit_solution(8992253339462172578)
XLA Ops:
  0.6 40.7 %shard_map.67 = (bf16[192,512]{1,0:T(8,128)(2,1)S(1)}, bf16[192,4096]{1,0:T(8,128)(2,1)S(1)}, bf16[128,512]{1,0:T(8,128)(2,1)S(1)}) custom-call(bf16[192,4096]{1,0:T(8,128)(2,1)} %tok_hbm.1, bf16[1024,512]{1,0:T(8,128)(2,1)} %quant_hbm.1, bf16[256]{0:T(256)(128)(2,1)} %scale_ref.1, bf16[192,512]{1,0:T(8,128)(2,1)} %kg_hbm.1), custom_call_target="tpu_custom_call" | custom-call | tf_op jit(solution)/shard_map/pallas_call | solution.py:422
  41.3 1.3 %shard_map.68 = (bf16[192,512]{1,0:T(8,128)(2,1)}, bf16[192,4096]{1,0:T(8,128)(2,1)}, bf16[128,512]{1,0:T(8,128)(2,1)}) custom-call(bf16[192,512]{1,0:T(8,128)(2,1)S(1)} %get-tuple-element.6.rot_in, bf16[192,4096]{1,0:T(8,128)(2,1)S(1)} %get-tuple-element.7.tg_in, bf16[128,512]{1,0:T(8,128)(2,1)S(1)} %get-tuple-element.8.wg_in), custom_call_target="tpu_custom_call" | custom-call | tf_op jit(solution)/shard_map/pallas_call | solution.py:455

commit v6 on v5

--- a/solution.py
+++ b/solution.py
@@ -335,6 +335,9 @@
     fb.launch(0, 1)
     pass_y(1)
     blocks(x, y)
+    fc.launch(0, 0)
+    fd.launch(0, 0)
+
     def dequant_other(i, carry):
         other = (2 * here + 2 + i) % 8
         dequant(other)
@@ -346,51 +349,50 @@
     pass_x(0)
     fa.take(0, 0)
     fb.take(0, 0)
-    for turn_of in range(2):
-        fc.launch(0, turn_of)
-        fd.launch(0, turn_of)
+    fc.launch(0, 1)
+    fd.launch(0, 1)
     pass_z(0)
-    pass_x(1)
     own.wait_recv()
     use(twin_shard, 0)
     use(twin_shard, 1)
-    pass_z(1)
+    pass_x(1)
     fa.take(0, 1)
     fb.take(0, 1)
+    pass_z(1)
     use(twin_shard, 2)
     use(twin_shard, 3)
     fa.take(1, 0)
     fb.take(1, 0)
     use(side, here)
-    pass_z(2)
     fc.take(0, 0)
     fd.take(0, 0)
     fa.take(1, 1)
     fb.take(1, 1)
-    pass_z(3)
+    pass_z(2)
     use(side, there_x)
-    use(side, there_z)
     fa.take(2, 0)
     fb.take(2, 0)
     fc.take(0, 1)
     fd.take(0, 1)
+    pass_z(3)
+    use(side, there_z)
+    fc.take(1, 0)
+    fd.take(1, 0)
     use(side, there)
+    fa.take(2, 1)
+    fb.take(2, 1)
     for copy in from_twin[:2]:
         copy.wait_recv()
     use(twin_side, here)
-    fc.take(1, 0)
-    fd.take(1, 0)
-    fa.take(2, 1)
-    fb.take(2, 1)
+    fc.take(1, 1)
+    fd.take(1, 1)
+    fc.take(2, 0)
+    fd.take(2, 0)
     for copy in from_twin[2:]:
         copy.wait_recv()
     use(twin_side, there_x)
     use(twin_side, there_z)
-    fc.take(1, 1)
-    fd.take(1, 1)
     use(twin_side, there)
-    fc.take(2, 0)
-    fd.take(2, 0)
     for h in range(heads):
         cols = slice(h * HEAD_DIM, (h + 1) * HEAD_DIM)
         rot_ref[:, cols] = turn(proj[:, cols], 0, 1.0).astype(jnp.bfloat16)

time: 42.7 us -> 43.8 us (1.026)
  Pallas kernels: 41.9 us -> 43 us
    pallas_call x1, Pallas kernels: 40.7 us -> 41.7 us  [fused_body(): pl.pallas_call(fused_kernel, out_shape=[pltpu.VMEM((row_count, width), bf...]
where the time goes in v6:
time: 43.8 us; the launch traced here: 43.6 us
  Pallas kernels  43 us (98%)
  between operations  0.64 us (1%)
    pallas_call x1, Pallas kernels, fused_body(): pl.pallas_call(fused_kernel, out_shape=[pltpu.VMEM((row_count, width), bf...  41.7 us
    pallas_call x1, Pallas kernels, fused_body(): pl.pallas_call(place_kernel, out_shape=[jax.ShapeDtypeStruct(value.shape,...  1.27 us

profile of v6, /device:TPU:0, one launch (start us, length us, event | category | flops | bytes accessed | tf_op | source)
XLA Modules:
  0.0 43.6 jit_solution(2872628249150184015)
XLA Ops:
  0.6 41.7 %shard_map.67 = (bf16[192,512]{1,0:T(8,128)(2,1)S(1)}, bf16[192,4096]{1,0:T(8,128)(2,1)S(1)}, bf16[128,512]{1,0:T(8,128)(2,1)S(1)}) custom-call(bf16[192,4096]{1,0:T(8,128)(2,1)} %tok_hbm.1, bf16[1024,512]{1,0:T(8,128)(2,1)} %quant_hbm.1, bf16[256]{0:T(256)(128)(2,1)} %scale_ref.1, bf16[192,512]{1,0:T(8,128)(2,1)} %kg_hbm.1), custom_call_target="tpu_custom_call" | custom-call | tf_op jit(solution)/shard_map/pallas_call | solution.py:424
  42.3 1.3 %shard_map.68 = (bf16[192,512]{1,0:T(8,128)(2,1)}, bf16[192,4096]{1,0:T(8,128)(2,1)}, bf16[128,512]{1,0:T(8,128)(2,1)}) custom-call(bf16[192,512]{1,0:T(8,128)(2,1)S(1)} %get-tuple-element.6.rot_in, bf16[192,4096]{1,0:T(8,128)(2,1)S(1)} %get-tuple-element.7.tg_in, bf16[128,512]{1,0:T(8,128)(2,1)S(1)} %get-tuple-element.8.wg_in), custom_call_target="tpu_custom_call" | custom-call | tf_op jit(solution)/shard_map/pallas_call | solution.py:457

commit v7 on v5

--- a/solution.py
+++ b/solution.py
@@ -150,6 +150,13 @@
             wbuf.at[shard, i], wbuf.at[shard, i], w_send.at[slot], w_recv.at[slot], to
         )
 
+    def w_copy(shard, i, slot, to):
+        return pltpu.make_async_remote_copy(
+            src_ref=wbuf.at[shard, i], dst_ref=wbuf.at[shard, i],
+            send_sem=w_send.at[slot], recv_sem=w_recv.at[slot],
+            device_id=to, device_id_type=MESH,
+        )
+
     from_y = [send_w(fsdp, 2 * here + q, q, over_y) for q in range(2)]
 
     def send_tokens(bx, by):
@@ -316,13 +323,33 @@
     def pass_x(q):
         i = 2 * there_x + q
         from_x[q].wait_recv()
-        from_z.append(send_w(side, i, 6 + q, over_z0))
-        from_twin.append(send_w(side, i, 10 + q, twin))
+        send_w(side, i, 10 + q, twin)
+
+        @pl.when(c == 1)
+        def _():
+            w_copy(side, i, 6 + q, over_z0).start()
+
+    def lift(q):
+        i = 2 * there_x + q
+
+        @pl.when(c == 1)
+        def _():
+            w_copy(twin_side, i, 10 + q, twin).wait_recv()
+            w_copy(twin_side, i, 17 + q, over_z0).start()
 
     def pass_z(q):
-        i = 2 * (there_z if q < 2 else there) + q % 2
         from_z[q].wait_recv()
-        from_twin.append(send_w(side, i, 12 + q, twin))
+        from_twin.append(send_w(side, 2 * there_z + q, 12 + q, twin))
+
+    def pass_z_both(q):
+        i = 2 * there + q
+
+        @pl.when(c == 1)
+        def _():
+            w_copy(side, i, 6 + q, over_z0).wait_recv()
+            w_copy(side, i, 14 + q, twin).start()
+            w_copy(twin_side, i, 17 + q, over_z0).wait_recv()
+            w_copy(twin_side, i, 19 + q, twin).start()
 
     proj[...] = jnp.zeros_like(proj)
     blocks(1 - x, 1 - y)
@@ -350,6 +377,7 @@
         fc.launch(0, turn_of)
         fd.launch(0, turn_of)
     pass_z(0)
+    lift(0)
     pass_x(1)
     own.wait_recv()
     use(twin_shard, 0)
@@ -357,24 +385,24 @@
     pass_z(1)
     fa.take(0, 1)
     fb.take(0, 1)
+    lift(1)
     use(twin_shard, 2)
     use(twin_shard, 3)
     fa.take(1, 0)
     fb.take(1, 0)
     use(side, here)
-    pass_z(2)
     fc.take(0, 0)
     fd.take(0, 0)
     fa.take(1, 1)
     fb.take(1, 1)
-    pass_z(3)
+    pass_z_both(0)
     use(side, there_x)
     use(side, there_z)
     fa.take(2, 0)
     fb.take(2, 0)
     fc.take(0, 1)
     fd.take(0, 1)
-    use(side, there)
+    pass_z_both(1)
     for copy in from_twin[:2]:
         copy.wait_recv()
     use(twin_side, here)
@@ -384,13 +412,22 @@
     fb.take(2, 1)
     for copy in from_twin[2:]:
         copy.wait_recv()
-    use(twin_side, there_x)
     use(twin_side, there_z)
     fc.take(1, 1)
     fd.take(1, 1)
-    use(twin_side, there)
     fc.take(2, 0)
     fd.take(2, 0)
+
+    @pl.when(c == 0)
+    def _():
+        for q in range(2):
+            w_copy(twin_side, 2 * there_x + q, 10 + q, twin).wait_recv()
+            w_copy(twin_side, 2 * there + q, 14 + q, twin).wait_recv()
+            w_copy(side, 2 * there + q, 19 + q, twin).wait_recv()
+
+    use(twin_side, there_x)
+    use(side, there)
+    use(twin_side, there)
     for h in range(heads):
         cols = slice(h * HEAD_DIM, (h + 1) * HEAD_DIM)
         rot_ref[:, cols] = turn(proj[:, cols], 0, 1.0).astype(jnp.bfloat16)
@@ -400,6 +437,14 @@
     fd.take(2, 1)
     fc.finish(slice(2 * quarter, 3 * quarter))
     fd.finish(slice(3 * quarter, block))
+
+    @pl.when(c == 1)
+    def _():
+        for q in range(2):
+            w_copy(side, 2 * there_x + q, 6 + q, over_z0).wait_send()
+            w_copy(twin_side, 2 * there_x + q, 17 + q, over_z0).wait_send()
+            w_copy(side, 2 * there + q, 14 + q, twin).wait_send()
+            w_copy(twin_side, 2 * there + q, 19 + q, twin).wait_send()
 
     for group in range(4):
         group_copy(group // 2, group % 2).wait_send()
@@ -443,8 +488,8 @@
             pltpu.SemaphoreType.DMA((3,)),
             pltpu.SemaphoreType.DMA((8,)),
             pltpu.SemaphoreType.DMA((2,)),
-            pltpu.SemaphoreType.DMA((17,)),
-            pltpu.SemaphoreType.DMA((17,)),
+            pltpu.SemaphoreType.DMA((21,)),
+            pltpu.SemaphoreType.DMA((21,)),
             pltpu.SemaphoreType.DMA((32,)),
             pltpu.SemaphoreType.DMA((32,)),
         ],

time: 42.7 us -> 44.1 us (1.033)
  Pallas kernels: 41.9 us -> 43.3 us
    pallas_call x1, Pallas kernels: 40.7 us -> 42 us  [fused_body(): pl.pallas_call(fused_kernel, out_shape=[pltpu.VMEM((row_count, width), bf...]
where the time goes in v7:
time: 44.1 us; the launch traced here: 43.9 us
  Pallas kernels  43.3 us (98%)
  between operations  0.64 us (1%)
    pallas_call x1, Pallas kernels, fused_body(): pl.pallas_call(fused_kernel, out_shape=[pltpu.VMEM((row_count, width), bf...  42 us
    pallas_call x1, Pallas kernels, fused_body(): pl.pallas_call(place_kernel, out_shape=[jax.ShapeDtypeStruct(value.shape,...  1.27 us

profile of v7, /device:TPU:0, one launch (start us, length us, event | category | flops | bytes accessed | tf_op | source)
XLA Modules:
  0.0 43.9 jit_solution(2334015343855947311)
XLA Ops:
  0.6 42.0 %shard_map.67 = (bf16[192,512]{1,0:T(8,128)(2,1)S(1)}, bf16[192,4096]{1,0:T(8,128)(2,1)S(1)}, bf16[128,512]{1,0:T(8,128)(2,1)S(1)}) custom-call(bf16[192,4096]{1,0:T(8,128)(2,1)} %tok_hbm.1, bf16[1024,512]{1,0:T(8,128)(2,1)} %quant_hbm.1, bf16[256]{0:T(256)(128)(2,1)} %scale_ref.1, bf16[192,512]{1,0:T(8,128)(2,1)} %kg_hbm.1), custom_call_target="tpu_custom_call" | custom-call | tf_op jit(solution)/shard_map/pallas_call | solution.py:467
  42.6 1.3 %shard_map.68 = (bf16[192,512]{1,0:T(8,128)(2,1)}, bf16[192,4096]{1,0:T(8,128)(2,1)}, bf16[128,512]{1,0:T(8,128)(2,1)}) custom-call(bf16[192,512]{1,0:T(8,128)(2,1)S(1)} %get-tuple-element.6.rot_in, bf16[192,4096]{1,0:T(8,128)(2,1)S(1)} %get-tuple-element.7.tg_in, bf16[128,512]{1,0:T(8,128)(2,1)S(1)} %get-tuple-element.8.wg_in), custom_call_target="tpu_custom_call" | custom-call | tf_op jit(solution)/shard_map/pallas_call | solution.py:500

commit v8 on v5

--- a/solution.py
+++ b/solution.py
@@ -331,9 +331,9 @@
     pass_y(0)
     blocks(1 - x, y)
     blocks(x, 1 - y)
+    pass_y(1)
     fa.launch(0, 1)
     fb.launch(0, 1)
-    pass_y(1)
     blocks(x, y)
     def dequant_other(i, carry):
         other = (2 * here + 2 + i) % 8
@@ -345,10 +345,9 @@
     use_all(fsdp)
     pass_x(0)
     fa.take(0, 0)
+    fc.launch(0, 0)
     fb.take(0, 0)
-    for turn_of in range(2):
-        fc.launch(0, turn_of)
-        fd.launch(0, turn_of)
+    fd.launch(0, 0)
     pass_z(0)
     pass_x(1)
     own.wait_recv()
@@ -356,7 +355,9 @@
     use(twin_shard, 1)
     pass_z(1)
     fa.take(0, 1)
+    fc.launch(0, 1)
     fb.take(0, 1)
+    fd.launch(0, 1)
     use(twin_shard, 2)
     use(twin_shard, 3)
     fa.take(1, 0)

time: 42.7 us -> 43.2 us (1.012)
  Pallas kernels: 41.9 us -> 42.4 us
where the time goes in v8:
time: 43.2 us; the launch traced here: 43 us
  Pallas kernels  42.4 us (98%)
  between operations  0.64 us (1%)
    pallas_call x1, Pallas kernels, fused_body(): pl.pallas_call(fused_kernel, out_shape=[pltpu.VMEM((row_count, width), bf...  41.1 us
    pallas_call x1, Pallas kernels, fused_body(): pl.pallas_call(place_kernel, out_shape=[jax.ShapeDtypeStruct(value.shape,...  1.27 us

profile of v8, /device:TPU:0, one launch (start us, length us, event | category | flops | bytes accessed | tf_op | source)
XLA Modules:
  0.0 43.0 jit_solution(94132493532292160)
XLA Ops:
  0.6 41.1 %shard_map.67 = (bf16[192,512]{1,0:T(8,128)(2,1)S(1)}, bf16[192,4096]{1,0:T(8,128)(2,1)S(1)}, bf16[128,512]{1,0:T(8,128)(2,1)S(1)}) custom-call(bf16[192,4096]{1,0:T(8,128)(2,1)} %tok_hbm.1, bf16[1024,512]{1,0:T(8,128)(2,1)} %quant_hbm.1, bf16[256]{0:T(256)(128)(2,1)} %scale_ref.1, bf16[192,512]{1,0:T(8,128)(2,1)} %kg_hbm.1), custom_call_target="tpu_custom_call" | custom-call | tf_op jit(solution)/shard_map/pallas_call | solution.py:423
  41.7 1.3 %shard_map.68 = (bf16[192,512]{1,0:T(8,128)(2,1)}, bf16[192,4096]{1,0:T(8,128)(2,1)}, bf16[128,512]{1,0:T(8,128)(2,1)}) custom-call(bf16[192,512]{1,0:T(8,128)(2,1)S(1)} %get-tuple-element.6.rot_in, bf16[192,4096]{1,0:T(8,128)(2,1)S(1)} %get-tuple-element.7.tg_in, bf16[128,512]{1,0:T(8,128)(2,1)S(1)} %get-tuple-element.8.wg_in), custom_call_target="tpu_custom_call" | custom-call | tf_op jit(solution)/shard_map/pallas_call | solution.py:456
